TPU v7x, 256 devices: a whole 4x4x8 slice. The times are simulated.
256 devices in a mesh: seq: 64 (over z_hi, x, y), dp: 4 (over z_lo, core).
Axes of the slice: x: 4, y: 4, z: 8 (z_hi: 4, z_lo: 2; z = z_hi * 2 + z_lo), core: 2. Of those that a mesh axis runs over, the one named last changes fastest.
Arguments:
- query_proj: bfloat16 [8, 512, 8192], P('dp', None, 'seq'), may hold values from -6 to 6
- key_proj: bfloat16 [8, 512, 8192], P('dp', None, 'seq'), may hold values from -6 to 6
- value_proj: bfloat16 [8, 512, 8192], P('dp', None, 'seq'), may hold values from -6 to 6
- long_filter: float32 [512, 8192], P(None, 'seq'), may hold values from -2 to 2
- skip_gain: float32 [512], replicated, may hold values from 0.25 to 1.5
- out_grad: bfloat16 [8, 512, 8192], P('dp', None, 'seq'), may hold values from -6 to 6
Outputs:
- output: bfloat16 [8, 512, 8192], P('dp', None, 'seq')
- grad_query: bfloat16 [8, 512, 8192], P('dp', None, 'seq')
- grad_key: bfloat16 [8, 512, 8192], P('dp', None, 'seq')
- grad_value: bfloat16 [8, 512, 8192], P('dp', None, 'seq')
- grad_filter: float32 [512, 8192], P(None, 'seq')
All inputs are finite; a program needn't handle non-finite values.
Results may differ from a plain program's by a relative error of at most 0.0014.
Values sent between devices are 32-bit elements; how exact they have to be, the bound alone decides.
No kernel may reach another device: no remote copies, remote signals or barrier semaphores. Data moves between devices by JAX's collectives and lax.ppermute only.
A program may use at most 64 MiB of HBM per device.

v0:
```python
import math

import jax
import jax.numpy as jnp
import numpy as np
from jax import lax
from jax.experimental import pallas as pl
from jax.experimental.pallas import tpu as pltpu
from jax.sharding import PartitionSpec as P

F32 = jnp.float32
BF16 = jnp.bfloat16
LANES = 128


def split_np(table):
    high = table.astype(jnp.bfloat16)
    low = (table - high.astype(np.float64)).astype(jnp.bfloat16)
    return high, low


def build_tables(half, scale):
    K1 = 2 * half
    total = K1 * LANES
    k1 = np.arange(K1)[:, None]
    n1 = np.arange(half)[None, :]
    ang = 2.0 * np.pi * ((k1 * n1) % K1) / K1
    c1, s1 = np.cos(ang), np.sin(ang)
    enter = np.block([[c1, s1], [-s1, c1]])
    enter_real = np.concatenate([c1, -s1], 0)
    n2 = np.arange(LANES)[:, None]
    k2 = np.arange(LANES)[None, :]
    ang2 = 2.0 * np.pi * ((n2 * k2) % LANES) / LANES
    c2, s2 = np.cos(ang2), np.sin(ang2)
    lane_fwd = np.block([[c2, -s2], [s2, c2]])
    lane_inv = np.block([[c2, s2], [-s2, c2]])
    leave = np.block([[c1.T, -s1.T], [s1.T, c1.T]]) / total
    leave_real = leave[:half] * scale
    phase = (np.arange(K1)[:, None] * np.arange(LANES)[None, :]) % total
    angt = 2.0 * np.pi * phase / total
    turn = np.concatenate([np.cos(angt), np.sin(angt)], 1).astype(np.float32)

    def left(table):
        high, low = split_np(table)
        return np.concatenate([high, high, low], 1)

    def right(table):
        high, low = split_np(table)
        return np.concatenate([high, high, low], 0)

    return (
        left(enter), left(enter_real), right(lane_fwd), right(lane_inv),
        left(leave), left(leave_real), turn,
    )


def parts(value, axis):
    high = value.astype(BF16)
    low = (value - high.astype(F32)).astype(BF16)
    return jnp.concatenate([high, low, high], axis)


def mm(a, b):
    return jnp.dot(a, b, preferred_element_type=F32)


def twist_forward(part, turn_cos, turn_sin):
    half = part.shape[0] // 2
    re, im = part[:half], part[half:]
    return jnp.concatenate(
        [re * turn_cos + im * turn_sin, im * turn_cos - re * turn_sin], 1
    )


def twist_back(part, turn_cos, turn_sin):
    re, im = part[:, :LANES], part[:, LANES:]
    return jnp.concatenate(
        [re * turn_cos - im * turn_sin, im * turn_cos + re * turn_sin], 0
    )


def pre_kernel(
    rows, own, core_ref, q_hbm, k_hbm, v_hbm, g_hbm, f_hbm, send_ref, q, k, v, g, f, hold, sems
):
    batch, chans = q.shape[0], q.shape[1]
    peers = chans // own
    copies = []
    for b in range(batch):
        for i, (src, dst) in enumerate(((k_hbm, k), (v_hbm, v), (g_hbm, g), (q_hbm, q))):
            copies.append(pltpu.make_async_copy(src.at[b], dst.at[b], sems.at[4 * b + i]))
    taps = pltpu.make_async_copy(f_hbm, f, sems.at[4 * batch])
    for copy in copies:
        copy.start()
    taps.start()
    for b in range(batch):
        for sig, (left, right) in enumerate(((k, v), (g, q))):
            copies[4 * b + 2 * sig].wait()
            copies[4 * b + 2 * sig + 1].wait()
            slot = hold.at[2 * b + sig]
            slot[...] = left[b].astype(F32) * right[b].astype(F32)
            for j in range(own):
                send_ref[pl.ds((sig * batch + b) * own + j, peers, stride=rows), :] = slot[
                    pl.ds(j, peers, stride=own), :
                ]
    taps.wait()
    send_ref[pl.ds(2 * batch * own, peers, stride=rows), :] = f[
        pl.ds(core_ref[0], peers, stride=own), :
    ]


def mid_kernel(
    devices, groups, own, batch, rows_in, rows_out, r_ref, enter, enter_real, lane_fwd, lane_inv,
    leave, leave_real, turn_ref, send_ref,
):
    turn_cos, turn_sin = turn_ref[:, :LANES], turn_ref[:, LANES:]
    K1 = 2 * devices
    pairs = 2 * groups
    for j in range(own):
        pieces = []
        for sig in range(2):
            for d in range(groups):
                base = d * rows_in + sig * batch * own + j
                re = r_ref[pl.ds(base, devices, stride=groups * rows_in), :]
                im = r_ref[pl.ds(base + own, devices, stride=groups * rows_in), :]
                pieces.append(jnp.concatenate([re, im], 0))
        taps = r_ref[
            pl.ds(j * rows_in + 2 * batch * own, devices, stride=groups * rows_in), :
        ]
        mid = mm(enter[...], parts(jnp.concatenate(pieces, 1), 0))
        turned = [
            twist_forward(mid[:, i * LANES : (i + 1) * LANES], turn_cos, turn_sin)
            for i in range(pairs)
        ]
        turned.append(twist_forward(mm(enter_real[...], parts(taps, 0)), turn_cos, turn_sin))
        spec = mm(parts(jnp.concatenate(turned, 0), 1), lane_fwd[...])
        hr, hi = spec[pairs * K1 :, :LANES], spec[pairs * K1 :, LANES:]
        products, backs = [], []
        cross_re = cross_im = 0.0
        for d in range(groups):
            mr, mi = spec[d * K1 : (d + 1) * K1, :LANES], spec[d * K1 : (d + 1) * K1, LANES:]
            at = (groups + d) * K1
            wr, wi = spec[at : at + K1, :LANES], spec[at : at + K1, LANES:]
            products.append(jnp.concatenate([mr * hr - mi * hi, mr * hi + mi * hr], 1))
            backs.append(jnp.concatenate([wr * hr + wi * hi, wi * hr - wr * hi], 1))
            cross_re = cross_re + (wr * mr + wi * mi)
            cross_im = cross_im + (wi * mr - wr * mi)
        cross = jnp.concatenate([cross_re, cross_im], 1)
        back = mm(parts(jnp.concatenate(products + backs + [cross], 0), 1), lane_inv[...])
        turned = [
            twist_back(back[i * K1 : (i + 1) * K1], turn_cos, turn_sin)
            for i in range(pairs + 1)
        ]
        final = mm(leave[...], parts(jnp.concatenate(turned[:pairs], 1), 0))
        terms = mm(leave_real[...], parts(turned[pairs], 0))
        for sig in range(2):
            for d in range(groups):
                col = (sig * groups + d) * LANES
                for b in range(batch):
                    base = d * rows_out + (sig * batch + b) * own + j
                    send_ref[pl.ds(base, devices, stride=groups * rows_out), :] = final[
                        b * devices : (b + 1) * devices, col : col + LANES
                    ]
        for d in range(groups):
            base = d * rows_out + 2 * batch * own + j
            send_ref[pl.ds(base, devices, stride=groups * rows_out), :] = terms


def post_kernel(
    rows, own, r_ref, skip_ref, q_ref, k_ref, v_ref, g_ref, out_ref, gq_ref, gk_ref, gv_ref,
    gf_ref, conv_ref, back_ref,
):
    batch, chans = q_ref.shape[0], q_ref.shape[1]
    peers = chans // own
    for j in range(own):
        gf_ref[pl.ds(j, peers, stride=own), :] = r_ref[
            pl.ds(2 * batch * own + j, peers, stride=rows), :
        ]
    skip = skip_ref[...]
    for b in range(batch):
        for j in range(own):
            conv_ref[pl.ds(j, peers, stride=own), :] = r_ref[
                pl.ds(b * own + j, peers, stride=rows), :
            ]
            back_ref[pl.ds(j, peers, stride=own), :] = r_ref[
                pl.ds((batch + b) * own + j, peers, stride=rows), :
            ]
        query, keys = q_ref[b].astype(F32), k_ref[b].astype(F32)
        values, upstream = v_ref[b].astype(F32), g_ref[b].astype(F32)
        gated = conv_ref[...] + skip * (keys * values)
        back = back_ref[...] + skip * (upstream * query)
        out_ref[b] = (query * gated).astype(BF16)
        gq_ref[b] = (upstream * gated).astype(BF16)
        gk_ref[b] = (back * values).astype(BF16)
        gv_ref[b] = (back * keys).astype(BF16)


VMEM = pl.BlockSpec(memory_space=pltpu.VMEM)
SMEM = pl.BlockSpec(memory_space=pltpu.SMEM)
HBM = pl.BlockSpec(memory_space=pltpu.HBM)
MIB = 1024 * 1024


def shards(devices, groups, tables, query_proj, key_proj, value_proj, long_filter, skip_gain, out_grad):
    batch, chans, cols = query_proj.shape
    peers = devices * groups
    own = chans // peers
    rows_in = 2 * batch * own + 1
    rows_out = 2 * batch * own + own
    core = lax.rem(lax.axis_index("dp"), own).astype(jnp.int32).reshape(1)

    def params(mib):
        return pltpu.CompilerParams(vmem_limit_bytes=mib * MIB)

    def exchange(flat, rows):
        shaped = flat.reshape(peers, rows, 1, cols)
        moved = lax.all_to_all(shaped, ("seq", "dp"), split_axis=0, concat_axis=0, tiled=True)
        return moved.reshape(peers * rows, cols)

    with jax.named_scope("pre"):
        wide = pltpu.VMEM((batch, chans, cols), BF16)
        send = pl.pallas_call(
            lambda *refs: pre_kernel(rows_in, own, *refs),
            out_shape=jax.ShapeDtypeStruct((peers * rows_in, cols), F32),
            in_specs=[SMEM] + [HBM] * 5,
            out_specs=VMEM,
            scratch_shapes=[
                wide, wide, wide, wide,
                pltpu.VMEM((chans, cols), F32),
                pltpu.VMEM((2 * batch, chans, cols), F32),
                pltpu.SemaphoreType.DMA((4 * batch + 1,)),
            ],
            compiler_params=params(48),
        )(core, query_proj, key_proj, value_proj, out_grad, long_filter)
    with jax.named_scope("gather"):
        arrived = exchange(send, rows_in)
    with jax.named_scope("mid"):
        send = pl.pallas_call(
            lambda *refs: mid_kernel(devices, groups, own, batch, rows_in, rows_out, *refs),
            out_shape=jax.ShapeDtypeStruct((peers * rows_out, cols), F32),
            in_specs=[VMEM] * (1 + len(tables)),
            out_specs=VMEM,
            compiler_params=params(48),
        )(arrived, *tables)
    with jax.named_scope("scatter"):
        returned = exchange(send, rows_out)
    with jax.named_scope("post"):
        plane = jax.ShapeDtypeStruct((batch, chans, cols), BF16)
        return pl.pallas_call(
            lambda *refs: post_kernel(rows_out, own, *refs),
            out_shape=[plane] * 4 + [jax.ShapeDtypeStruct((chans, cols), F32)],
            in_specs=[VMEM] * 6,
            out_specs=[VMEM] * 5,
            scratch_shapes=[pltpu.VMEM((chans, cols), F32)] * 2,
            compiler_params=params(48),
        )(returned, skip_gain[:, None], query_proj, key_proj, value_proj, out_grad)


def solution(mesh):
    devices, groups = mesh.shape["seq"], mesh.shape["dp"]
    tables = build_tables(devices, 1.0 / math.sqrt(2 * groups * devices * LANES))

    def run(*args):
        return tuple(shards(devices, groups, tables, *args))

    wide = P("dp", None, "seq")
    return jax.shard_map(
        run,
        mesh=mesh,
        in_specs=(wide, wide, wide, P(None, "seq"), P(), wide),
        out_specs=(wide, wide, wide, wide, P(None, "seq")),
        check_vma=False,
    )
```

profile of v0, /device:TPU:1, one launch (start us, length us, event | category | flops | bytes accessed | tf_op | source)
XLA Modules:
  0.0 108.4 jit_solution(3228432187807674510)
XLA Ops:
  0.6 0.0 copy-start
  0.6 0.9 copy-done
  1.6 0.0 copy-start.2
  1.6 0.9 copy-done.2
  2.5 0.0 copy-start.4
  2.5 0.9 copy-done.4
  3.5 0.0 copy-start.6
  3.5 0.9 copy-done.6
  4.4 0.0 copy-start.10
  4.4 0.9 copy-done.10
  5.4 1.7 %pre.1 = f32[2304,128]{1,0:T(8,128)S(1)} custom-call(s32[1]{0:T(128)} %bitcast.refs_0_, bf16[2,512,128]{2,1,0:T(8,128)(2,1)S(1)} %copy-done, bf16[2,512,128]{2,1,0:T(8,128)(2,1)S(1)} %copy-done.2, bf16[2,512,128]{2,1,0:T(8,128)(2,1)S(1)} %copy-done.4, bf16[2,512,128]{2,1,0:T(8,128)(2,1)S(1)} %copy-done.6, f32[512,128]{1,0:T(8,128)S(1)} %copy-done.10), custom_call_target="tpu_custom_call" | custom-call | tf_op jit(solution)/shard_map/pre/pallas_call | solution.py:221
  7.1 0.0 copy-start.8
  7.1 0.0 copy-start.9
  7.1 0.0 copy-start.11
  7.1 0.0 copy-start.12
  7.1 0.0 copy-start.13
  7.2 0.0 copy-start.14
  7.2 0.0 copy-start.15
  7.2 50.7 %all_to_all.10 = f32[256,9,1,128]{3,2,1,0:T(1,128)S(1)} all-to-all(f32[256,9,1,128]{3,2,1,0:T(1,128)S(1)} %bitcast.7), channel_id=1, replica_groups=mesh['seq'=64,'dp'=4] {'seq','dp'}, dimensions={0} | all-to-all | bytes 2359296 | tf_op jit(solution)/shard_map/gather/all_to_all | solution.py:216
  57.8 0.0 copy-done.8
  57.8 0.0 copy-done.9
  57.8 0.0 copy-done.11
  57.8 0.0 copy-done.12
  57.9 0.0 copy-done.13
  57.9 0.0 copy-done.14
  57.9 0.0 copy-done.15
  57.9 6.2 %mid.1 = f32[2560,128]{1,0:T(8,128)} custom-call(f32[2304,128]{1,0:T(8,128)S(1)} %bitcast.8, bf16[256,384]{1,0:T(8,128)(2,1)S(1)} %copy-done.11, bf16[256,192]{1,0:T(8,128)(2,1)S(1)} %copy-done.13, bf16[768,256]{1,0:T(8,128)(2,1)S(1)} %copy-done.8, bf16[768,256]{1,0:T(8,128)(2,1)S(1)} %copy-done.9, bf16[128,768]{1,0:T(8,128)(2,1)S(1)} %copy-done.12, ...), custom_call_target="tpu_custom_call" | custom-call | tf_op jit(solution)/shard_map/mid/pallas_call | solution.py:237
  64.1 0.0 copy-start.16
  64.1 0.0 copy-start.1
  64.1 0.0 copy-start.3
  64.1 0.0 copy-start.5
  64.1 0.0 copy-start.7
  64.2 5.3 %all-to-all-start.1 = ((f32[256,10,1,128]{3,2,1,0:T(1,128)}), f32[256,10,1,128]{3,2,1,0:T(1,128)S(1)}, u32[]{:S(2)}, u32[]{:S(2)}) async-start(f32[256,10,1,128]{3,2,1,0:T(1,128)} %bitcast.3), calls=%async_computation.1 | async-start | bytes 2621440 | tf_op jit(solution)/shard_map/scatter/all_to_all | solution.py:216
  69.5 0.0 copy-done.16
  69.5 0.1 copy.21.refs_1_
  69.6 37.2 %all-to-all-done.1 = f32[256,10,1,128]{3,2,1,0:T(1,128)S(1)} async-done(((f32[256,10,1,128]{3,2,1,0:T(1,128)}), f32[256,10,1,128]{3,2,1,0:T(1,128)S(1)}, u32[]{:S(2)}, u32[]{:S(2)}) %all-to-all-start.1) | async-done | bytes 1310752 | tf_op jit(solution)/shard_map/scatter/all_to_all | solution.py:216
  106.9 0.0 copy-done.1
  106.9 0.0 copy-done.3
  106.9 0.0 copy-done.5
  106.9 0.0 copy-done.7
  106.9 1.5 %post.1 = (bf16[2,512,128]{2,1,0:T(8,128)(2,1)}, bf16[2,512,128]{2,1,0:T(8,128)(2,1)}, bf16[2,512,128]{2,1,0:T(8,128)(2,1)}, bf16[2,512,128]{2,1,0:T(8,128)(2,1)}, f32[512,128]{1,0:T(8,128)}) custom-call(f32[2560,128]{1,0:T(8,128)S(1)} %bitcast.6, f32[512,1]{1,0:T(8,128)S(1)} %copy.21.refs_1_, bf16[2,512,128]{2,1,0:T(8,128)(2,1)S(1)} %copy-done.1, ...), custom_call_target="tpu_custom_call" | custom-call | tf_op jit(solution)/shard_map/post/pallas_call | solution.py:248
Async XLA Ops:
  0.6 1.0 copy-start
  1.6 0.9 copy-start.2
  2.5 0.9 copy-start.4
  3.5 0.9 copy-start.6
  4.4 0.9 copy-start.10
  7.1 50.7 %copy-start.8 = (bf16[768,256]{1,0:T(8,128)(2,1)S(1)}, bf16[768,256]{1,0:T(8,128)(2,1)}, u32[]{:S(2)}) copy-start(bf16[768,256]{1,0:T(8,128)(2,1)} %constant.25.clone.refs_3_) | copy-start | bytes 1179652
  7.1 50.7 %copy-start.9 = (bf16[768,256]{1,0:T(8,128)(2,1)S(1)}, bf16[768,256]{1,0:T(8,128)(2,1)}, u32[]{:S(2)}) copy-start(bf16[768,256]{1,0:T(8,128)(2,1)} %constant.26.clone.refs_4_) | copy-start | bytes 1179652
  7.1 50.7 %copy-start.11 = (bf16[256,384]{1,0:T(8,128)(2,1)S(1)}, bf16[256,384]{1,0:T(8,128)(2,1)}, u32[]{:S(2)}) copy-start(bf16[256,384]{1,0:T(8,128)(2,1)} %constant.23.clone.refs_1_) | copy-start | bytes 589828
  7.1 50.7 %copy-start.12 = (bf16[128,768]{1,0:T(8,128)(2,1)S(1)}, bf16[128,768]{1,0:T(8,128)(2,1)}, u32[]{:S(2)}) copy-start(bf16[128,768]{1,0:T(8,128)(2,1)} %constant.27.clone.refs_5_) | copy-start | bytes 589828
  7.1 50.7 %copy-start.13 = (bf16[256,192]{1,0:T(8,128)(2,1)S(1)}, bf16[256,192]{1,0:T(8,128)(2,1)}, u32[]{:S(2)}) copy-start(bf16[256,192]{1,0:T(8,128)(2,1)} %constant.24.clone.refs_2_) | copy-start | bytes 294916
  7.2 50.7 %copy-start.14 = (f32[128,256]{1,0:T(8,128)S(1)}, f32[128,256]{1,0:T(8,128)}, u32[]{:S(2)}) copy-start(f32[128,256]{1,0:T(8,128)} %constant.29.clone.refs_7_) | copy-start | bytes 393220
  7.2 50.7 %copy-start.15 = (bf16[64,768]{1,0:T(8,128)(2,1)S(1)}, bf16[64,768]{1,0:T(8,128)(2,1)}, u32[]{:S(2)}) copy-start(bf16[64,768]{1,0:T(8,128)(2,1)} %constant.28.clone.refs_6_) | copy-start | bytes 294916
  64.1 5.4 %copy-start.16 = (f32[512]{0:T(512)S(1)}, f32[512]{0:T(512)}, u32[]{:S(2)}) copy-start(f32[512]{0:T(512)} %param.17) | copy-start | bytes 6148
  64.1 42.8 %copy-start.1 = (bf16[2,512,128]{2,1,0:T(8,128)(2,1)S(1)}, bf16[2,512,128]{2,1,0:T(8,128)(2,1)}, u32[]{:S(2)}) copy-start(bf16[2,512,128]{2,1,0:T(8,128)(2,1)} %refs_2_.4) | copy-start | bytes 786436
  64.1 42.8 %copy-start.3 = (bf16[2,512,128]{2,1,0:T(8,128)(2,1)S(1)}, bf16[2,512,128]{2,1,0:T(8,128)(2,1)}, u32[]{:S(2)}) copy-start(bf16[2,512,128]{2,1,0:T(8,128)(2,1)} %refs_3_.4) | copy-start | bytes 786436
  64.1 42.8 %copy-start.5 = (bf16[2,512,128]{2,1,0:T(8,128)(2,1)S(1)}, bf16[2,512,128]{2,1,0:T(8,128)(2,1)}, u32[]{:S(2)}) copy-start(bf16[2,512,128]{2,1,0:T(8,128)(2,1)} %refs_4_.4) | copy-start | bytes 786436
  64.1 42.8 %copy-start.7 = (bf16[2,512,128]{2,1,0:T(8,128)(2,1)S(1)}, bf16[2,512,128]{2,1,0:T(8,128)(2,1)}, u32[]{:S(2)}) copy-start(bf16[2,512,128]{2,1,0:T(8,128)(2,1)} %refs_5_.4) | copy-start | bytes 786436
  64.2 42.7 %all-to-all-start.1 = ((f32[256,10,1,128]{3,2,1,0:T(1,128)}), f32[256,10,1,128]{3,2,1,0:T(1,128)S(1)}, u32[]{:S(2)}, u32[]{:S(2)}) async-start(f32[256,10,1,128]{3,2,1,0:T(1,128)} %bitcast.3), calls=%async_computation.1 | async-start | bytes 2621440 | tf_op jit(solution)/shard_map/scatter/all_to_all | solution.py:216
where the time goes:
time: 109 us; the launch traced here: 108 us
  blocking collectives  50.7 us (47%)
  waiting for transfers between devices  37.2 us (34%)
  Pallas kernels  9.44 us (9%)
  starting transfers between devices  5.32 us (5%)
  local copies, waits for them, and re-layouts  4.96 us (5%)
    all_to_all x1, blocking collectives, exchange(): lax.all_to_all(shaped, ('seq', 'dp'), split_axis=0, concat_axis=0, tiled=...  50.7 us
    all_to_all x1, waiting for transfers between devices, exchange(): lax.all_to_all(shaped, ('seq', 'dp'), split_axis=0, concat_axis=0, tiled=...  37.2 us
    pallas_call x1, Pallas kernels, shards(): pl.pallas_call(lambda *refs: mid_kernel(devices, groups, own, batch, rows...  6.25 us
    all_to_all x1, starting transfers between devices, exchange(): lax.all_to_all(shaped, ('seq', 'dp'), split_axis=0, concat_axis=0, tiled=...  5.32 us
    unnamed x34, local copies, waits for them, and re-layouts  4.81 us
  transfers between devices with their start and end apart: 1, of which 1 were waited for; matrix products, arithmetic and copies ran while one was open for 0% of the time, Pallas kernels for 0%

commit v1 on v0

--- a/solution.py
+++ b/solution.py
@@ -108,73 +108,89 @@
     ]
 
 
+def leave_product(table, data):
+    depth = data.shape[0]
+    high = data.astype(BF16)
+    low = (data - high.astype(F32)).astype(BF16)
+    first = table[:, :depth]
+    return mm(first, high) + mm(first, low) + mm(table[:, 2 * depth :], high)
+
+
 def mid_kernel(
     devices, groups, own, batch, rows_in, rows_out, r_ref, enter, enter_real, lane_fwd, lane_inv,
     leave, leave_real, turn_ref, send_ref,
 ):
     turn_cos, turn_sin = turn_ref[:, :LANES], turn_ref[:, LANES:]
     K1 = 2 * devices
-    pairs = 2 * groups
+    step_in, step_out = groups * rows_in, groups * rows_out
+
+    def lanes(value, i):
+        return value[:, i * LANES : (i + 1) * LANES]
+
+    pieces = []
     for j in range(own):
-        pieces = []
         for sig in range(2):
             for d in range(groups):
                 base = d * rows_in + sig * batch * own + j
-                re = r_ref[pl.ds(base, devices, stride=groups * rows_in), :]
-                im = r_ref[pl.ds(base + own, devices, stride=groups * rows_in), :]
+                re = r_ref[pl.ds(base, devices, stride=step_in), :]
+                im = r_ref[pl.ds(base + own, devices, stride=step_in), :]
                 pieces.append(jnp.concatenate([re, im], 0))
-        taps = r_ref[
-            pl.ds(j * rows_in + 2 * batch * own, devices, stride=groups * rows_in), :
-        ]
-        mid = mm(enter[...], parts(jnp.concatenate(pieces, 1), 0))
-        turned = [
-            twist_forward(mid[:, i * LANES : (i + 1) * LANES], turn_cos, turn_sin)
-            for i in range(pairs)
-        ]
-        turned.append(twist_forward(mm(enter_real[...], parts(taps, 0)), turn_cos, turn_sin))
-        spec = mm(parts(jnp.concatenate(turned, 0), 1), lane_fwd[...])
-        hr, hi = spec[pairs * K1 :, :LANES], spec[pairs * K1 :, LANES:]
-        products, backs = [], []
+    taps = [
+        r_ref[pl.ds(j * rows_in + 2 * batch * own, devices, stride=step_in), :]
+        for j in range(own)
+    ]
+    count = len(pieces)
+    real = mm(enter_real[...], parts(jnp.concatenate(taps, 1), 0))
+    full = mm(enter[...], parts(jnp.concatenate(pieces, 1), 0))
+    turned = [twist_forward(lanes(real, j), turn_cos, turn_sin) for j in range(own)]
+    turned += [twist_forward(lanes(full, i), turn_cos, turn_sin) for i in range(count)]
+    spec = mm(parts(jnp.concatenate(turned, 0), 1), lane_fwd[...])
+
+    def pair(i):
+        rows = spec[i * K1 : (i + 1) * K1]
+        return rows[:, :LANES], rows[:, LANES:]
+
+    products, crosses = [], []
+    for j in range(own):
+        hr, hi = pair(j)
         cross_re = cross_im = 0.0
+        conv, back = [], []
         for d in range(groups):
-            mr, mi = spec[d * K1 : (d + 1) * K1, :LANES], spec[d * K1 : (d + 1) * K1, LANES:]
-            at = (groups + d) * K1
-            wr, wi = spec[at : at + K1, :LANES], spec[at : at + K1, LANES:]
-            products.append(jnp.concatenate([mr * hr - mi * hi, mr * hi + mi * hr], 1))
-            backs.append(jnp.concatenate([wr * hr + wi * hi, wi * hr - wr * hi], 1))
+            mr, mi = pair(own + 2 * j * groups + d)
+            wr, wi = pair(own + (2 * j + 1) * groups + d)
+            conv.append(jnp.concatenate([mr * hr - mi * hi, mr * hi + mi * hr], 1))
+            back.append(jnp.concatenate([wr * hr + wi * hi, wi * hr - wr * hi], 1))
             cross_re = cross_re + (wr * mr + wi * mi)
             cross_im = cross_im + (wi * mr - wr * mi)
-        cross = jnp.concatenate([cross_re, cross_im], 1)
-        back = mm(parts(jnp.concatenate(products + backs + [cross], 0), 1), lane_inv[...])
-        turned = [
-            twist_back(back[i * K1 : (i + 1) * K1], turn_cos, turn_sin)
-            for i in range(pairs + 1)
-        ]
-        final = mm(leave[...], parts(jnp.concatenate(turned[:pairs], 1), 0))
-        terms = mm(leave_real[...], parts(turned[pairs], 0))
+        products += conv + back
+        crosses.append(jnp.concatenate([cross_re, cross_im], 1))
+    spread = mm(parts(jnp.concatenate(products + crosses, 0), 1), lane_inv[...])
+    turned = [
+        twist_back(spread[i * K1 : (i + 1) * K1], turn_cos, turn_sin)
+        for i in range(count + own)
+    ]
+    final = leave_product(leave[...], jnp.concatenate(turned[:count], 1))
+    terms = leave_product(leave_real[...], jnp.concatenate(turned[count:], 1))
+    for j in range(own):
         for sig in range(2):
             for d in range(groups):
-                col = (sig * groups + d) * LANES
+                part = lanes(final, (2 * j + sig) * groups + d)
                 for b in range(batch):
                     base = d * rows_out + (sig * batch + b) * own + j
-                    send_ref[pl.ds(base, devices, stride=groups * rows_out), :] = final[
-                        b * devices : (b + 1) * devices, col : col + LANES
+                    send_ref[pl.ds(base, devices, stride=step_out), :] = part[
+                        b * devices : (b + 1) * devices
                     ]
-        for d in range(groups):
-            base = d * rows_out + 2 * batch * own + j
-            send_ref[pl.ds(base, devices, stride=groups * rows_out), :] = terms
+        for d in range(j, groups, own):
+            base = d * rows_out + 2 * batch * own
+            send_ref[pl.ds(base, devices, stride=step_out), :] = lanes(terms, j)
 
 
 def post_kernel(
     rows, own, r_ref, skip_ref, q_ref, k_ref, v_ref, g_ref, out_ref, gq_ref, gk_ref, gv_ref,
-    gf_ref, conv_ref, back_ref,
+    conv_ref, back_ref,
 ):
     batch, chans = q_ref.shape[0], q_ref.shape[1]
     peers = chans // own
-    for j in range(own):
-        gf_ref[pl.ds(j, peers, stride=own), :] = r_ref[
-            pl.ds(2 * batch * own + j, peers, stride=rows), :
-        ]
     skip = skip_ref[...]
     for b in range(batch):
         for j in range(own):
@@ -194,6 +210,13 @@
         gv_ref[b] = (back * keys).astype(BF16)
 
 
+def join_kernel(own, core_ref, mine_ref, other_ref, out_ref):
+    peers = mine_ref.shape[0]
+    core = core_ref[0]
+    out_ref[pl.ds(core, peers, stride=own), :] = mine_ref[...]
+    out_ref[pl.ds(own - 1 - core, peers, stride=own), :] = other_ref[...]
+
+
 VMEM = pl.BlockSpec(memory_space=pltpu.VMEM)
 SMEM = pl.BlockSpec(memory_space=pltpu.SMEM)
 HBM = pl.BlockSpec(memory_space=pltpu.HBM)
@@ -205,7 +228,7 @@
     peers = devices * groups
     own = chans // peers
     rows_in = 2 * batch * own + 1
-    rows_out = 2 * batch * own + own
+    rows_out = rows_in
     core = lax.rem(lax.axis_index("dp"), own).astype(jnp.int32).reshape(1)
 
     def params(mib):
@@ -229,7 +252,7 @@
                 pltpu.VMEM((2 * batch, chans, cols), F32),
                 pltpu.SemaphoreType.DMA((4 * batch + 1,)),
             ],
-            compiler_params=params(48),
+            compiler_params=params(62),
         )(core, query_proj, key_proj, value_proj, out_grad, long_filter)
     with jax.named_scope("gather"):
         arrived = exchange(send, rows_in)
@@ -242,17 +265,33 @@
             compiler_params=params(48),
         )(arrived, *tables)
     with jax.named_scope("scatter"):
-        returned = exchange(send, rows_out)
+        shaped = send.reshape(peers, rows_out, 1, cols)
+        returned = lax.all_to_all(shaped, ("seq", "dp"), split_axis=0, concat_axis=0, tiled=True)
+    with jax.named_scope("swap"):
+        mine = returned[:, rows_out - 1].reshape(peers, cols)
+        pairs = [(d, d + 1 - 2 * (d % own)) for d in range(groups)]
+        other = lax.ppermute(mine, "dp", pairs)
     with jax.named_scope("post"):
         plane = jax.ShapeDtypeStruct((batch, chans, cols), BF16)
-        return pl.pallas_call(
+        planes = pl.pallas_call(
             lambda *refs: post_kernel(rows_out, own, *refs),
-            out_shape=[plane] * 4 + [jax.ShapeDtypeStruct((chans, cols), F32)],
+            out_shape=[plane] * 4,
             in_specs=[VMEM] * 6,
-            out_specs=[VMEM] * 5,
+            out_specs=[VMEM] * 4,
             scratch_shapes=[pltpu.VMEM((chans, cols), F32)] * 2,
             compiler_params=params(48),
-        )(returned, skip_gain[:, None], query_proj, key_proj, value_proj, out_grad)
+            cost_estimate=pl.CostEstimate(flops=10**6, bytes_accessed=4 * 10**6, transcendentals=0),
+        )(returned.reshape(peers * rows_out, cols), skip_gain[:, None], query_proj, key_proj, value_proj, out_grad)
+    with jax.named_scope("join"):
+        grad_filter = pl.pallas_call(
+            lambda *refs: join_kernel(own, *refs),
+            out_shape=jax.ShapeDtypeStruct((chans, cols), F32),
+            in_specs=[SMEM, VMEM, VMEM],
+            out_specs=VMEM,
+            compiler_params=params(48),
+            cost_estimate=pl.CostEstimate(flops=10**5, bytes_accessed=5 * 10**5, transcendentals=0),
+        )(core, mine, other)
+    return (*planes, grad_filter)
 
 
 def solution(mesh):
@@ -260,7 +299,7 @@
     tables = build_tables(devices, 1.0 / math.sqrt(2 * groups * devices * LANES))
 
     def run(*args):
-        return tuple(shards(devices, groups, tables, *args))
+        return shards(devices, groups, tables, *args)
 
     wide = P("dp", None, "seq")
     return jax.shard_map(

time: 109 us -> 101 us (0.927)
  blocking collectives: 50.7 us -> 90.6 us
  waiting for transfers between devices: 37.2 us -> 0.01 us
  starting transfers between devices: 5.32 us -> 0.09 us
  local copies, waits for them, and re-layouts: 4.96 us -> 0.31 us
    all_to_all x0 -> x1, blocking collectives: none -> 39.7 us  [shards(): lax.all_to_all(shaped, ('seq', 'dp'), split_axis=0, concat_axis=0, tiled=...]
    all_to_all x1 -> x0, waiting for transfers between devices: 37.2 us -> none  [exchange(): lax.all_to_all(shaped, ('seq', 'dp'), split_axis=0, concat_axis=0, tiled=...]
    all_to_all x1 -> x0, starting transfers between devices: 5.32 us -> none  [exchange(): lax.all_to_all(shaped, ('seq', 'dp'), split_axis=0, concat_axis=0, tiled=...]
    unnamed x34 -> x24, local copies, waits for them, and re-layouts: 4.81 us -> 0.08 us
    pallas_call x1, Pallas kernels: 6.25 us -> 4.61 us  [shards(): pl.pallas_call(lambda *refs: mid_kernel(devices, groups, own, batch, rows...]
  transfers between devices with their start and end apart: 1 -> 1, of which waited for: 1 -> 0; matrix products, arithmetic and copies ran while one was open for 0% -> 0% of each run, Pallas kernels for 0% -> 1%
where the time goes in v1:
time: 101 us
  blocking collectives  90.6 us (90%)
  Pallas kernels  9.23 us (9%)
    all_to_all x1, blocking collectives, exchange(): lax.all_to_all(shaped, ('seq', 'dp'), split_axis=0, concat_axis=0, tiled=...  50.9 us
    all_to_all x1, blocking collectives, shards(): lax.all_to_all(shaped, ('seq', 'dp'), split_axis=0, concat_axis=0, tiled=...  39.7 us
    pallas_call x1, Pallas kernels, shards(): pl.pallas_call(lambda *refs: mid_kernel(devices, groups, own, batch, rows...  4.61 us
    pallas_call x1, Pallas kernels, shards(): pl.pallas_call(lambda *refs: pre_kernel(rows_in, own, *refs), out_shape=j...  2.49 us
  transfers between devices with their start and end apart: 1, of which 0 were waited for; matrix products, arithmetic and copies ran while one was open for 0% of the time, Pallas kernels for 1%

profile of v1, /device:TPU:1, one launch (start us, length us, event | category | flops | bytes accessed | tf_op | source)
XLA Modules:
  0.0 101.1 jit_solution(2221766100710042472)
XLA Ops:
  0.6 2.5 %pre.1 = f32[2304,128]{1,0:T(8,128)} custom-call(s32[1]{0:T(128)} %bitcast.refs_0_, bf16[2,512,128]{2,1,0:T(8,128)(2,1)} %refs_2_.4, bf16[2,512,128]{2,1,0:T(8,128)(2,1)} %refs_3_.4, bf16[2,512,128]{2,1,0:T(8,128)(2,1)} %refs_4_.4, bf16[2,512,128]{2,1,0:T(8,128)(2,1)} %refs_5_.4, f32[512,128]{1,0:T(8,128)} %refs_5_.3), custom_call_target="tpu_custom_call" | custom-call | tf_op jit(solution)/shard_map/pre/pallas_call | solution.py:244
  3.1 0.0 copy-start.4
  3.1 0.0 copy-start.5
  3.2 0.0 copy-start.6
  3.2 0.0 copy-start.7
  3.2 0.0 copy-start.8
  3.2 0.0 copy-start.9
  3.2 0.0 copy-start.10
  3.2 50.9 %all_to_all.10 = f32[256,9,1,128]{3,2,1,0:T(1,128)S(1)} all-to-all(f32[256,9,1,128]{3,2,1,0:T(1,128)} %bitcast.14), channel_id=1, replica_groups=mesh['seq'=64,'dp'=4] {'seq','dp'}, dimensions={0} | all-to-all | bytes 2359296 | tf_op jit(solution)/shard_map/gather/all_to_all | solution.py:239
  54.1 0.0 copy-done.4
  54.1 0.0 copy-done.5
  54.1 0.0 copy-done.6
  54.1 0.0 copy-done.7
  54.1 0.0 copy-done.8
  54.1 0.0 copy-done.9
  54.1 0.0 copy-done.10
  54.1 4.6 %mid.1 = f32[2304,128]{1,0:T(8,128)S(1)} custom-call(f32[2304,128]{1,0:T(8,128)S(1)} %bitcast.10, bf16[256,384]{1,0:T(8,128)(2,1)S(1)} %copy-done.6, bf16[256,192]{1,0:T(8,128)(2,1)S(1)} %copy-done.8, bf16[768,256]{1,0:T(8,128)(2,1)S(1)} %copy-done.4, bf16[768,256]{1,0:T(8,128)(2,1)S(1)} %copy-done.5, bf16[128,768]{1,0:T(8,128)(2,1)S(1)} %copy-done.7, ...), custom_call_target="tpu_custom_call" | custom-call | tf_op jit(solution)/shard_map/mid/pallas_call | solution.py:260
  58.8 0.0 copy-start.11
  58.8 0.0 copy-start
  58.8 0.0 copy-start.1
  58.8 0.0 copy-start.2
  58.8 0.0 copy-start.3
  58.8 39.7 %all_to_all.11 = f32[256,9,1,128]{3,2,1,0:T(1,128)S(1)} all-to-all(f32[256,9,1,128]{3,2,1,0:T(1,128)S(1)} %bitcast.11), channel_id=1, replica_groups=mesh['seq'=64,'dp'=4] {'seq','dp'}, dimensions={0} | all-to-all | bytes 2359296 | tf_op jit(solution)/shard_map/scatter/all_to_all | solution.py:269
  98.6 0.1 slice.4
  98.7 0.1 collective-permute-start
  98.8 0.0 copy-done.11
  98.8 0.1 copy.23.refs_1_
  98.9 0.0 copy-done
  98.9 0.0 copy-done.1
  98.9 0.0 copy-done.2
  98.9 0.0 copy-done.3
  99.0 1.4 %post.1 = (bf16[2,512,128]{2,1,0:T(8,128)(2,1)}, bf16[2,512,128]{2,1,0:T(8,128)(2,1)}, bf16[2,512,128]{2,1,0:T(8,128)(2,1)}, bf16[2,512,128]{2,1,0:T(8,128)(2,1)}) custom-call(f32[2304,128]{1,0:T(8,128)S(1)} %bitcast.9, f32[512,1]{1,0:T(8,128)S(1)} %copy.23.refs_1_, bf16[2,512,128]{2,1,0:T(8,128)(2,1)S(1)} %copy-done, bf16[2,512,128]{2,1,0:T(8,128)(2,1)S(1)} %copy-done.1, ...), custom_call_target="tpu_custom_call" | custom-call | flops 1000000 | bytes 4000000 | tf_op jit(solution)/shard_map/post/pallas_call | solution.py:276
  100.4 0.0 collective-permute-done.refs_2_
  100.4 0.7 join.1
Async XLA Ops:
  3.1 51.0 %copy-start.4 = (bf16[768,256]{1,0:T(8,128)(2,1)S(1)}, bf16[768,256]{1,0:T(8,128)(2,1)}, u32[]{:S(2)}) copy-start(bf16[768,256]{1,0:T(8,128)(2,1)} %constant.25.clone.refs_3_) | copy-start | bytes 1179652
  3.1 51.0 %copy-start.5 = (bf16[768,256]{1,0:T(8,128)(2,1)S(1)}, bf16[768,256]{1,0:T(8,128)(2,1)}, u32[]{:S(2)}) copy-start(bf16[768,256]{1,0:T(8,128)(2,1)} %constant.26.clone.refs_4_) | copy-start | bytes 1179652
  3.2 50.9 %copy-start.6 = (bf16[256,384]{1,0:T(8,128)(2,1)S(1)}, bf16[256,384]{1,0:T(8,128)(2,1)}, u32[]{:S(2)}) copy-start(bf16[256,384]{1,0:T(8,128)(2,1)} %constant.23.clone.refs_1_) | copy-start | bytes 589828
  3.2 50.9 %copy-start.7 = (bf16[128,768]{1,0:T(8,128)(2,1)S(1)}, bf16[128,768]{1,0:T(8,128)(2,1)}, u32[]{:S(2)}) copy-start(bf16[128,768]{1,0:T(8,128)(2,1)} %constant.27.clone.refs_5_) | copy-start | bytes 589828
  3.2 50.9 %copy-start.8 = (bf16[256,192]{1,0:T(8,128)(2,1)S(1)}, bf16[256,192]{1,0:T(8,128)(2,1)}, u32[]{:S(2)}) copy-start(bf16[256,192]{1,0:T(8,128)(2,1)} %constant.24.clone.refs_2_) | copy-start | bytes 294916
  3.2 50.9 %copy-start.9 = (f32[128,256]{1,0:T(8,128)S(1)}, f32[128,256]{1,0:T(8,128)}, u32[]{:S(2)}) copy-start(f32[128,256]{1,0:T(8,128)} %constant.29.clone.refs_7_) | copy-start | bytes 393220
  3.2 50.9 %copy-start.10 = (bf16[64,768]{1,0:T(8,128)(2,1)S(1)}, bf16[64,768]{1,0:T(8,128)(2,1)}, u32[]{:S(2)}) copy-start(bf16[64,768]{1,0:T(8,128)(2,1)} %constant.28.clone.refs_6_) | copy-start | bytes 294916
  58.8 40.0 %copy-start.11 = (f32[512]{0:T(512)S(1)}, f32[512]{0:T(512)}, u32[]{:S(2)}) copy-start(f32[512]{0:T(512)} %param.17) | copy-start | bytes 6148
  58.8 40.2 %copy-start = (bf16[2,512,128]{2,1,0:T(8,128)(2,1)S(1)}, bf16[2,512,128]{2,1,0:T(8,128)(2,1)}, u32[]{:S(2)}) copy-start(bf16[2,512,128]{2,1,0:T(8,128)(2,1)} %refs_2_.4) | copy-start | bytes 786436
  58.8 40.2 %copy-start.1 = (bf16[2,512,128]{2,1,0:T(8,128)(2,1)S(1)}, bf16[2,512,128]{2,1,0:T(8,128)(2,1)}, u32[]{:S(2)}) copy-start(bf16[2,512,128]{2,1,0:T(8,128)(2,1)} %refs_3_.4) | copy-start | bytes 786436
  58.8 40.1 %copy-start.2 = (bf16[2,512,128]{2,1,0:T(8,128)(2,1)S(1)}, bf16[2,512,128]{2,1,0:T(8,128)(2,1)}, u32[]{:S(2)}) copy-start(bf16[2,512,128]{2,1,0:T(8,128)(2,1)} %refs_4_.4) | copy-start | bytes 786436
  58.8 40.1 %copy-start.3 = (bf16[2,512,128]{2,1,0:T(8,128)(2,1)S(1)}, bf16[2,512,128]{2,1,0:T(8,128)(2,1)}, u32[]{:S(2)}) copy-start(bf16[2,512,128]{2,1,0:T(8,128)(2,1)} %refs_5_.4) | copy-start | bytes 786436
  98.7 1.7 %collective-permute-start = (f32[256,128]{1,0:T(8,128)S(1)}, f32[256,128]{1,0:T(8,128)S(1)}, u32[]{:S(2)}, u32[]{:S(2)}) collective-permute-start(f32[256,128]{1,0:T(8,128)S(1)} %bitcast.12), channel_id=1, source_target_pairs={{0,1},{1,0},{2,3},{3,2},{4,5},{5,4},{6,7},{7,6},{8,9},{9,8},{10,11... | collective-permute-start | bytes 393224 | tf_op jit(solution)/shard_map/swap/ppermute | solution.py:273

commit v2 on v1

--- a/solution.py
+++ b/solution.py
@@ -11,6 +11,7 @@
 F32 = jnp.float32
 BF16 = jnp.bfloat16
 LANES = 128
+CHUNKS = 4
 
 
 def split_np(table):
@@ -80,32 +81,44 @@
 
 
 def pre_kernel(
-    rows, own, core_ref, q_hbm, k_hbm, v_hbm, g_hbm, f_hbm, send_ref, q, k, v, g, f, hold, sems
+    rows, own, core_ref, q_hbm, k_hbm, v_hbm, g_hbm, f_hbm, send_hbm, q, k, v, g, f, send, hold,
+    sems, out_sems,
 ):
     batch, chans = q.shape[0], q.shape[1]
-    peers = chans // own
+    span = chans // CHUNKS
+    peers = span // own
     copies = []
-    for b in range(batch):
+    for n in range(CHUNKS):
+        part = pl.ds(n * span, span)
         for i, (src, dst) in enumerate(((k_hbm, k), (v_hbm, v), (g_hbm, g), (q_hbm, q))):
-            copies.append(pltpu.make_async_copy(src.at[b], dst.at[b], sems.at[4 * b + i]))
-    taps = pltpu.make_async_copy(f_hbm, f, sems.at[4 * batch])
+            copies.append(
+                pltpu.make_async_copy(src.at[:, part], dst.at[:, part], sems.at[5 * n + i])
+            )
+        copies.append(pltpu.make_async_copy(f_hbm.at[part], f.at[part], sems.at[5 * n + 4]))
     for copy in copies:
         copy.start()
-    taps.start()
-    for b in range(batch):
+    sent = []
+    for n in range(CHUNKS):
+        part = pl.ds(n * span, span)
+        base = n * peers * rows
         for sig, (left, right) in enumerate(((k, v), (g, q))):
-            copies[4 * b + 2 * sig].wait()
-            copies[4 * b + 2 * sig + 1].wait()
-            slot = hold.at[2 * b + sig]
-            slot[...] = left[b].astype(F32) * right[b].astype(F32)
-            for j in range(own):
-                send_ref[pl.ds((sig * batch + b) * own + j, peers, stride=rows), :] = slot[
-                    pl.ds(j, peers, stride=own), :
-                ]
-    taps.wait()
-    send_ref[pl.ds(2 * batch * own, peers, stride=rows), :] = f[
-        pl.ds(core_ref[0], peers, stride=own), :
-    ]
+            copies[5 * n + 2 * sig].wait()
+            copies[5 * n + 2 * sig + 1].wait()
+            for b in range(batch):
+                slot = hold.at[(2 * n + sig) * batch + b]
+                slot[...] = left[b, part].astype(F32) * right[b, part].astype(F32)
+                for j in range(own):
+                    at = base + (sig * batch + b) * own + j
+                    send[pl.ds(at, peers, stride=rows), :] = slot[pl.ds(j, peers, stride=own), :]
+        copies[5 * n + 4].wait()
+        send[pl.ds(base + 2 * batch * own, peers, stride=rows), :] = f[
+            pl.ds(n * span + core_ref[0], peers, stride=own), :
+        ]
+        block = pl.ds(base, peers * rows)
+        sent.append(pltpu.make_async_copy(send.at[block], send_hbm.at[block], out_sems.at[n]))
+        sent[n].start()
+    for copy in sent:
+        copy.wait()
 
 
 def leave_product(table, data):
@@ -186,28 +199,37 @@
 
 
 def post_kernel(
-    rows, own, r_ref, skip_ref, q_ref, k_ref, v_ref, g_ref, out_ref, gq_ref, gk_ref, gv_ref,
-    conv_ref, back_ref,
+    rows, own, r_ref, skip_ref, q_ref, k_ref, v_ref, g_ref, out_hbm, gq_hbm, gk_hbm, gv_hbm,
+    out, gq, gk, gv, conv_ref, back_ref, sems,
 ):
     batch, chans = q_ref.shape[0], q_ref.shape[1]
-    peers = chans // own
-    skip = skip_ref[...]
-    for b in range(batch):
-        for j in range(own):
-            conv_ref[pl.ds(j, peers, stride=own), :] = r_ref[
-                pl.ds(b * own + j, peers, stride=rows), :
-            ]
-            back_ref[pl.ds(j, peers, stride=own), :] = r_ref[
-                pl.ds((batch + b) * own + j, peers, stride=rows), :
-            ]
-        query, keys = q_ref[b].astype(F32), k_ref[b].astype(F32)
-        values, upstream = v_ref[b].astype(F32), g_ref[b].astype(F32)
-        gated = conv_ref[...] + skip * (keys * values)
-        back = back_ref[...] + skip * (upstream * query)
-        out_ref[b] = (query * gated).astype(BF16)
-        gq_ref[b] = (upstream * gated).astype(BF16)
-        gk_ref[b] = (back * values).astype(BF16)
-        gv_ref[b] = (back * keys).astype(BF16)
+    span = chans // CHUNKS
+    peers = span // own
+    sent = []
+    for n in range(CHUNKS):
+        part = pl.ds(n * span, span)
+        skip = skip_ref[part, :]
+        for b in range(batch):
+            conv, back = conv_ref.at[n * batch + b], back_ref.at[n * batch + b]
+            for j in range(own):
+                at = n * peers * rows + b * own + j
+                conv[pl.ds(j, peers, stride=own), :] = r_ref[pl.ds(at, peers, stride=rows), :]
+                at += batch * own
+                back[pl.ds(j, peers, stride=own), :] = r_ref[pl.ds(at, peers, stride=rows), :]
+            query, keys = q_ref[b, part].astype(F32), k_ref[b, part].astype(F32)
+            values, upstream = v_ref[b, part].astype(F32), g_ref[b, part].astype(F32)
+            gated = conv[...] + skip * (keys * values)
+            total = back[...] + skip * (upstream * query)
+            out[b, part] = (query * gated).astype(BF16)
+            gq[b, part] = (upstream * gated).astype(BF16)
+            gk[b, part] = (total * values).astype(BF16)
+            gv[b, part] = (total * keys).astype(BF16)
+        for i, (src, dst) in enumerate(((out, out_hbm), (gq, gq_hbm), (gk, gk_hbm), (gv, gv_hbm))):
+            copy = pltpu.make_async_copy(src.at[:, part], dst.at[:, part], sems.at[4 * n + i])
+            copy.start()
+            sent.append(copy)
+    for copy in sent:
+        copy.wait()
 
 
 def join_kernel(own, core_ref, mine_ref, other_ref, out_ref):
@@ -245,12 +267,14 @@
             lambda *refs: pre_kernel(rows_in, own, *refs),
             out_shape=jax.ShapeDtypeStruct((peers * rows_in, cols), F32),
             in_specs=[SMEM] + [HBM] * 5,
-            out_specs=VMEM,
+            out_specs=HBM,
             scratch_shapes=[
                 wide, wide, wide, wide,
                 pltpu.VMEM((chans, cols), F32),
-                pltpu.VMEM((2 * batch, chans, cols), F32),
-                pltpu.SemaphoreType.DMA((4 * batch + 1,)),
+                pltpu.VMEM((peers * rows_in, cols), F32),
+                pltpu.VMEM((2 * batch * CHUNKS, chans // CHUNKS, cols), F32),
+                pltpu.SemaphoreType.DMA((5 * CHUNKS,)),
+                pltpu.SemaphoreType.DMA((CHUNKS,)),
             ],
             compiler_params=params(62),
         )(core, query_proj, key_proj, value_proj, out_grad, long_filter)
@@ -277,8 +301,10 @@
             lambda *refs: post_kernel(rows_out, own, *refs),
             out_shape=[plane] * 4,
             in_specs=[VMEM] * 6,
-            out_specs=[VMEM] * 4,
-            scratch_shapes=[pltpu.VMEM((chans, cols), F32)] * 2,
+            out_specs=[HBM] * 4,
+            scratch_shapes=[wide] * 4
+            + [pltpu.VMEM((batch * CHUNKS, chans // CHUNKS, cols), F32)] * 2
+            + [pltpu.SemaphoreType.DMA((4 * CHUNKS,))],
             compiler_params=params(48),
             cost_estimate=pl.CostEstimate(flops=10**6, bytes_accessed=4 * 10**6, transcendentals=0),
         )(returned.reshape(peers * rows_out, cols), skip_gain[:, None], query_proj, key_proj, value_proj, out_grad)

time: 101 us -> 101 us (level)
  no operation moved by 1% of the time
where the time goes in v2:
time: 101 us
  blocking collectives  90.6 us (90%)
  Pallas kernels  8.85 us (9%)
    all_to_all x1, blocking collectives, exchange(): lax.all_to_all(shaped, ('seq', 'dp'), split_axis=0, concat_axis=0, tiled=...  50.9 us
    all_to_all x1, blocking collectives, shards(): lax.all_to_all(shaped, ('seq', 'dp'), split_axis=0, concat_axis=0, tiled=...  39.8 us
    pallas_call x1, Pallas kernels, shards(): pl.pallas_call(lambda *refs: mid_kernel(devices, groups, own, batch, rows...  4.61 us
    pallas_call x1, Pallas kernels, shards(): pl.pallas_call(lambda *refs: pre_kernel(rows_in, own, *refs), out_shape=j...  2.27 us
  transfers between devices with their start and end apart: 1, of which 0 were waited for; matrix products, arithmetic and copies ran while one was open for 0% of the time, Pallas kernels for 1%

profile of v2, /device:TPU:1, one launch (start us, length us, event | category | flops | bytes accessed | tf_op | source)
XLA Modules:
  0.0 100.7 jit_solution(11929133663300999594)
XLA Ops:
  0.6 2.3 %pre.1 = f32[2304,128]{1,0:T(8,128)} custom-call(s32[1]{0:T(128)} %bitcast.refs_0_, bf16[2,512,128]{2,1,0:T(8,128)(2,1)} %refs_2_.4, bf16[2,512,128]{2,1,0:T(8,128)(2,1)} %refs_3_.4, bf16[2,512,128]{2,1,0:T(8,128)(2,1)} %refs_4_.4, bf16[2,512,128]{2,1,0:T(8,128)(2,1)} %refs_5_.4, f32[512,128]{1,0:T(8,128)} %refs_5_.3), custom_call_target="tpu_custom_call" | custom-call | tf_op jit(solution)/shard_map/pre/pallas_call | solution.py:266
  2.9 0.0 copy-start.4
  2.9 0.0 copy-start.5
  2.9 0.0 copy-start.6
  3.0 0.0 copy-start.7
  3.0 0.0 copy-start.8
  3.0 0.0 copy-start.9
  3.0 0.0 copy-start.10
  3.0 50.9 %all_to_all.10 = f32[256,9,1,128]{3,2,1,0:T(1,128)S(1)} all-to-all(f32[256,9,1,128]{3,2,1,0:T(1,128)} %bitcast.14), channel_id=1, replica_groups=mesh['seq'=64,'dp'=4] {'seq','dp'}, dimensions={0} | all-to-all | bytes 2359296 | tf_op jit(solution)/shard_map/gather/all_to_all | solution.py:261
  53.9 0.0 copy-done.4
  53.9 0.0 copy-done.5
  53.9 0.0 copy-done.6
  53.9 0.0 copy-done.7
  53.9 0.0 copy-done.8
  53.9 0.0 copy-done.9
  53.9 0.0 copy-done.10
  53.9 4.6 %mid.1 = f32[2304,128]{1,0:T(8,128)S(1)} custom-call(f32[2304,128]{1,0:T(8,128)S(1)} %bitcast.10, bf16[256,384]{1,0:T(8,128)(2,1)S(1)} %copy-done.6, bf16[256,192]{1,0:T(8,128)(2,1)S(1)} %copy-done.8, bf16[768,256]{1,0:T(8,128)(2,1)S(1)} %copy-done.4, bf16[768,256]{1,0:T(8,128)(2,1)S(1)} %copy-done.5, bf16[128,768]{1,0:T(8,128)(2,1)S(1)} %copy-done.7, ...), custom_call_target="tpu_custom_call" | custom-call | tf_op jit(solution)/shard_map/mid/pallas_call | solution.py:284
  58.5 0.0 copy-start.11
  58.5 0.0 copy-start
  58.6 0.0 copy-start.1
  58.6 0.0 copy-start.2
  58.6 0.0 copy-start.3
  58.6 39.8 %all_to_all.11 = f32[256,9,1,128]{3,2,1,0:T(1,128)S(1)} all-to-all(f32[256,9,1,128]{3,2,1,0:T(1,128)S(1)} %bitcast.11), channel_id=1, replica_groups=mesh['seq'=64,'dp'=4] {'seq','dp'}, dimensions={0} | all-to-all | bytes 2359296 | tf_op jit(solution)/shard_map/scatter/all_to_all | solution.py:293
  98.3 0.1 slice.4
  98.4 0.1 collective-permute-start
  98.5 0.0 copy-done.11
  98.6 0.1 copy.23.refs_1_
  98.7 0.0 copy-done
  98.7 0.0 copy-done.1
  98.7 0.0 copy-done.2
  98.7 0.0 copy-done.3
  98.7 1.2 %post.1 = (bf16[2,512,128]{2,1,0:T(8,128)(2,1)}, bf16[2,512,128]{2,1,0:T(8,128)(2,1)}, bf16[2,512,128]{2,1,0:T(8,128)(2,1)}, bf16[2,512,128]{2,1,0:T(8,128)(2,1)}) custom-call(f32[2304,128]{1,0:T(8,128)S(1)} %bitcast.9, f32[512,1]{1,0:T(8,128)S(1)} %copy.23.refs_1_, bf16[2,512,128]{2,1,0:T(8,128)(2,1)S(1)} %copy-done, bf16[2,512,128]{2,1,0:T(8,128)(2,1)S(1)} %copy-done.1, ...), custom_call_target="tpu_custom_call" | custom-call | flops 1000000 | bytes 4000000 | tf_op jit(solution)/shard_map/post/pallas_call | solution.py:300
  100.0 0.0 collective-permute-done.refs_2_
  100.0 0.7 join.1
Async XLA Ops:
  2.9 51.0 %copy-start.4 = (bf16[768,256]{1,0:T(8,128)(2,1)S(1)}, bf16[768,256]{1,0:T(8,128)(2,1)}, u32[]{:S(2)}) copy-start(bf16[768,256]{1,0:T(8,128)(2,1)} %constant.25.clone.refs_3_) | copy-start | bytes 1179652
  2.9 51.0 %copy-start.5 = (bf16[768,256]{1,0:T(8,128)(2,1)S(1)}, bf16[768,256]{1,0:T(8,128)(2,1)}, u32[]{:S(2)}) copy-start(bf16[768,256]{1,0:T(8,128)(2,1)} %constant.26.clone.refs_4_) | copy-start | bytes 1179652
  2.9 50.9 %copy-start.6 = (bf16[256,384]{1,0:T(8,128)(2,1)S(1)}, bf16[256,384]{1,0:T(8,128)(2,1)}, u32[]{:S(2)}) copy-start(bf16[256,384]{1,0:T(8,128)(2,1)} %constant.23.clone.refs_1_) | copy-start | bytes 589828
  3.0 50.9 %copy-start.7 = (bf16[128,768]{1,0:T(8,128)(2,1)S(1)}, bf16[128,768]{1,0:T(8,128)(2,1)}, u32[]{:S(2)}) copy-start(bf16[128,768]{1,0:T(8,128)(2,1)} %constant.27.clone.refs_5_) | copy-start | bytes 589828
  3.0 50.9 %copy-start.8 = (bf16[256,192]{1,0:T(8,128)(2,1)S(1)}, bf16[256,192]{1,0:T(8,128)(2,1)}, u32[]{:S(2)}) copy-start(bf16[256,192]{1,0:T(8,128)(2,1)} %constant.24.clone.refs_2_) | copy-start | bytes 294916
  3.0 50.9 %copy-start.9 = (f32[128,256]{1,0:T(8,128)S(1)}, f32[128,256]{1,0:T(8,128)}, u32[]{:S(2)}) copy-start(f32[128,256]{1,0:T(8,128)} %constant.29.clone.refs_7_) | copy-start | bytes 393220
  3.0 50.9 %copy-start.10 = (bf16[64,768]{1,0:T(8,128)(2,1)S(1)}, bf16[64,768]{1,0:T(8,128)(2,1)}, u32[]{:S(2)}) copy-start(bf16[64,768]{1,0:T(8,128)(2,1)} %constant.28.clone.refs_6_) | copy-start | bytes 294916
  58.5 40.0 %copy-start.11 = (f32[512]{0:T(512)S(1)}, f32[512]{0:T(512)}, u32[]{:S(2)}) copy-start(f32[512]{0:T(512)} %param.17) | copy-start | bytes 6148
  58.5 40.2 %copy-start = (bf16[2,512,128]{2,1,0:T(8,128)(2,1)S(1)}, bf16[2,512,128]{2,1,0:T(8,128)(2,1)}, u32[]{:S(2)}) copy-start(bf16[2,512,128]{2,1,0:T(8,128)(2,1)} %refs_2_.4) | copy-start | bytes 786436
  58.6 40.2 %copy-start.1 = (bf16[2,512,128]{2,1,0:T(8,128)(2,1)S(1)}, bf16[2,512,128]{2,1,0:T(8,128)(2,1)}, u32[]{:S(2)}) copy-start(bf16[2,512,128]{2,1,0:T(8,128)(2,1)} %refs_3_.4) | copy-start | bytes 786436
  58.6 40.2 %copy-start.2 = (bf16[2,512,128]{2,1,0:T(8,128)(2,1)S(1)}, bf16[2,512,128]{2,1,0:T(8,128)(2,1)}, u32[]{:S(2)}) copy-start(bf16[2,512,128]{2,1,0:T(8,128)(2,1)} %refs_4_.4) | copy-start | bytes 786436
  58.6 40.2 %copy-start.3 = (bf16[2,512,128]{2,1,0:T(8,128)(2,1)S(1)}, bf16[2,512,128]{2,1,0:T(8,128)(2,1)}, u32[]{:S(2)}) copy-start(bf16[2,512,128]{2,1,0:T(8,128)(2,1)} %refs_5_.4) | copy-start | bytes 786436
  98.4 1.6 %collective-permute-start = (f32[256,128]{1,0:T(8,128)S(1)}, f32[256,128]{1,0:T(8,128)S(1)}, u32[]{:S(2)}, u32[]{:S(2)}) collective-permute-start(f32[256,128]{1,0:T(8,128)S(1)} %bitcast.12), channel_id=1, source_target_pairs={{0,1},{1,0},{2,3},{3,2},{4,5},{5,4},{6,7},{7,6},{8,9},{9,8},{10,11... | collective-permute-start | bytes 393224 | tf_op jit(solution)/shard_map/swap/ppermute | solution.py:297

commit v3 on v2

--- a/solution.py
+++ b/solution.py
@@ -140,59 +140,66 @@
     def lanes(value, i):
         return value[:, i * LANES : (i + 1) * LANES]
 
-    pieces = []
-    for j in range(own):
-        for sig in range(2):
-            for d in range(groups):
-                base = d * rows_in + sig * batch * own + j
-                re = r_ref[pl.ds(base, devices, stride=step_in), :]
-                im = r_ref[pl.ds(base + own, devices, stride=step_in), :]
-                pieces.append(jnp.concatenate([re, im], 0))
+    def load(j, sig, d):
+        base = d * rows_in + sig * batch * own + j
+        re = r_ref[pl.ds(base, devices, stride=step_in), :]
+        im = r_ref[pl.ds(base + own, devices, stride=step_in), :]
+        return jnp.concatenate([re, im], 0)
+
+    def forward(value, count):
+        turned = [twist_forward(lanes(value, i), turn_cos, turn_sin) for i in range(count)]
+        return mm(parts(jnp.concatenate(turned, 0), 1), lane_fwd[...])
+
+    def inverse(spread, table, count):
+        turned = [
+            twist_back(spread[i * K1 : (i + 1) * K1], turn_cos, turn_sin) for i in range(count)
+        ]
+        return leave_product(table[...], jnp.concatenate(turned, 1))
+
+    def pair(spec, i):
+        rows = spec[i * K1 : (i + 1) * K1]
+        return rows[:, :LANES], rows[:, LANES:]
+
+    count = 2 * groups
     taps = [
         r_ref[pl.ds(j * rows_in + 2 * batch * own, devices, stride=step_in), :]
         for j in range(own)
     ]
-    count = len(pieces)
     real = mm(enter_real[...], parts(jnp.concatenate(taps, 1), 0))
-    full = mm(enter[...], parts(jnp.concatenate(pieces, 1), 0))
-    turned = [twist_forward(lanes(real, j), turn_cos, turn_sin) for j in range(own)]
-    turned += [twist_forward(lanes(full, i), turn_cos, turn_sin) for i in range(count)]
-    spec = mm(parts(jnp.concatenate(turned, 0), 1), lane_fwd[...])
-
-    def pair(i):
-        rows = spec[i * K1 : (i + 1) * K1]
-        return rows[:, :LANES], rows[:, LANES:]
-
-    products, crosses = [], []
+    taps_spec = forward(real, own)
+    loaded = [
+        jnp.concatenate([load(j, sig, d) for sig in range(2) for d in range(groups)], 1)
+        for j in range(own)
+    ]
+    entered = [mm(enter[...], parts(value, 0)) for value in loaded]
+    specs = [forward(value, count) for value in entered]
+    spreads, crosses = [], []
     for j in range(own):
-        hr, hi = pair(j)
+        hr, hi = pair(taps_spec, j)
         cross_re = cross_im = 0.0
         conv, back = [], []
         for d in range(groups):
-            mr, mi = pair(own + 2 * j * groups + d)
-            wr, wi = pair(own + (2 * j + 1) * groups + d)
+            mr, mi = pair(specs[j], d)
+            wr, wi = pair(specs[j], groups + d)
             conv.append(jnp.concatenate([mr * hr - mi * hi, mr * hi + mi * hr], 1))
             back.append(jnp.concatenate([wr * hr + wi * hi, wi * hr - wr * hi], 1))
             cross_re = cross_re + (wr * mr + wi * mi)
             cross_im = cross_im + (wi * mr - wr * mi)
-        products += conv + back
+        spreads.append(mm(parts(jnp.concatenate(conv + back, 0), 1), lane_inv[...]))
         crosses.append(jnp.concatenate([cross_re, cross_im], 1))
-    spread = mm(parts(jnp.concatenate(products + crosses, 0), 1), lane_inv[...])
-    turned = [
-        twist_back(spread[i * K1 : (i + 1) * K1], turn_cos, turn_sin)
-        for i in range(count + own)
-    ]
-    final = leave_product(leave[...], jnp.concatenate(turned[:count], 1))
-    terms = leave_product(leave_real[...], jnp.concatenate(turned[count:], 1))
+    cross_spread = mm(parts(jnp.concatenate(crosses, 0), 1), lane_inv[...])
     for j in range(own):
+        final = inverse(spreads[j], leave, count)
         for sig in range(2):
             for d in range(groups):
-                part = lanes(final, (2 * j + sig) * groups + d)
+                part = lanes(final, sig * groups + d)
                 for b in range(batch):
                     base = d * rows_out + (sig * batch + b) * own + j
                     send_ref[pl.ds(base, devices, stride=step_out), :] = part[
                         b * devices : (b + 1) * devices
                     ]
+    terms = inverse(cross_spread, leave_real, own)
+    for j in range(own):
         for d in range(j, groups, own):
             base = d * rows_out + 2 * batch * own
             send_ref[pl.ds(base, devices, stride=step_out), :] = lanes(terms, j)

time: 101 us -> 99.9 us (0.989)
  Pallas kernels: 8.85 us -> 7.77 us
    pallas_call x1, Pallas kernels: 4.61 us -> 3.52 us  [shards(): pl.pallas_call(lambda *refs: mid_kernel(devices, groups, own, batch, rows...]
where the time goes in v3:
time: 99.9 us; the launch traced here: 99.6 us
  blocking collectives  90.6 us (91%)
  Pallas kernels  7.77 us (8%)
    all_to_all x1, blocking collectives, exchange(): lax.all_to_all(shaped, ('seq', 'dp'), split_axis=0, concat_axis=0, tiled=...  50.9 us
    all_to_all x1, blocking collectives, shards(): lax.all_to_all(shaped, ('seq', 'dp'), split_axis=0, concat_axis=0, tiled=...  39.7 us
    pallas_call x1, Pallas kernels, shards(): pl.pallas_call(lambda *refs: mid_kernel(devices, groups, own, batch, rows...  3.52 us
    pallas_call x1, Pallas kernels, shards(): pl.pallas_call(lambda *refs: pre_kernel(rows_in, own, *refs), out_shape=j...  2.27 us
  transfers between devices with their start and end apart: 1, of which 0 were waited for; matrix products, arithmetic and copies ran while one was open for 0% of the time, Pallas kernels for 1%

profile of v3, /device:TPU:1, one launch (start us, length us, event | category | flops | bytes accessed | tf_op | source)
XLA Modules:
  0.0 99.6 jit_solution(15278656216529625147)
XLA Ops:
  0.6 2.3 %pre.1 = f32[2304,128]{1,0:T(8,128)} custom-call(s32[1]{0:T(128)} %bitcast.refs_0_, bf16[2,512,128]{2,1,0:T(8,128)(2,1)} %refs_2_.4, bf16[2,512,128]{2,1,0:T(8,128)(2,1)} %refs_3_.4, bf16[2,512,128]{2,1,0:T(8,128)(2,1)} %refs_4_.4, bf16[2,512,128]{2,1,0:T(8,128)(2,1)} %refs_5_.4, f32[512,128]{1,0:T(8,128)} %refs_5_.3), custom_call_target="tpu_custom_call" | custom-call | tf_op jit(solution)/shard_map/pre/pallas_call | solution.py:273
  2.9 0.0 copy-start.4
  2.9 0.0 copy-start.5
  2.9 0.0 copy-start.6
  3.0 0.0 copy-start.7
  3.0 0.0 copy-start.8
  3.0 0.0 copy-start.9
  3.0 0.0 copy-start.10
  3.0 50.9 %all_to_all.10 = f32[256,9,1,128]{3,2,1,0:T(1,128)S(1)} all-to-all(f32[256,9,1,128]{3,2,1,0:T(1,128)} %bitcast.14), channel_id=1, replica_groups=mesh['seq'=64,'dp'=4] {'seq','dp'}, dimensions={0} | all-to-all | bytes 2359296 | tf_op jit(solution)/shard_map/gather/all_to_all | solution.py:268
  53.9 0.0 copy-done.4
  53.9 0.0 copy-done.5
  53.9 0.0 copy-done.6
  53.9 0.0 copy-done.7
  53.9 0.0 copy-done.8
  53.9 0.0 copy-done.9
  53.9 0.0 copy-done.10
  53.9 3.5 %mid.1 = f32[2304,128]{1,0:T(8,128)S(1)} custom-call(f32[2304,128]{1,0:T(8,128)S(1)} %bitcast.10, bf16[256,384]{1,0:T(8,128)(2,1)S(1)} %copy-done.6, bf16[256,192]{1,0:T(8,128)(2,1)S(1)} %copy-done.8, bf16[768,256]{1,0:T(8,128)(2,1)S(1)} %copy-done.4, bf16[768,256]{1,0:T(8,128)(2,1)S(1)} %copy-done.5, bf16[128,768]{1,0:T(8,128)(2,1)S(1)} %copy-done.7, ...), custom_call_target="tpu_custom_call" | custom-call | tf_op jit(solution)/shard_map/mid/pallas_call | solution.py:291
  57.4 0.0 copy-start.11
  57.5 0.0 copy-start
  57.5 0.0 copy-start.1
  57.5 0.0 copy-start.2
  57.5 0.0 copy-start.3
  57.5 39.7 %all_to_all.11 = f32[256,9,1,128]{3,2,1,0:T(1,128)S(1)} all-to-all(f32[256,9,1,128]{3,2,1,0:T(1,128)S(1)} %bitcast.11), channel_id=1, replica_groups=mesh['seq'=64,'dp'=4] {'seq','dp'}, dimensions={0} | all-to-all | bytes 2359296 | tf_op jit(solution)/shard_map/scatter/all_to_all | solution.py:300
  97.3 0.1 slice.4
  97.3 0.1 collective-permute-start
  97.4 0.0 copy-done.11
  97.5 0.1 copy.23.refs_1_
  97.6 0.0 copy-done
  97.6 0.0 copy-done.1
  97.6 0.0 copy-done.2
  97.6 0.0 copy-done.3
  97.7 1.2 %post.1 = (bf16[2,512,128]{2,1,0:T(8,128)(2,1)}, bf16[2,512,128]{2,1,0:T(8,128)(2,1)}, bf16[2,512,128]{2,1,0:T(8,128)(2,1)}, bf16[2,512,128]{2,1,0:T(8,128)(2,1)}) custom-call(f32[2304,128]{1,0:T(8,128)S(1)} %bitcast.9, f32[512,1]{1,0:T(8,128)S(1)} %copy.23.refs_1_, bf16[2,512,128]{2,1,0:T(8,128)(2,1)S(1)} %copy-done, bf16[2,512,128]{2,1,0:T(8,128)(2,1)S(1)} %copy-done.1, ...), custom_call_target="tpu_custom_call" | custom-call | flops 1000000 | bytes 4000000 | tf_op jit(solution)/shard_map/post/pallas_call | solution.py:307
  98.9 0.0 collective-permute-done.refs_2_
  98.9 0.7 join.1
Async XLA Ops:
  2.9 51.0 %copy-start.4 = (bf16[768,256]{1,0:T(8,128)(2,1)S(1)}, bf16[768,256]{1,0:T(8,128)(2,1)}, u32[]{:S(2)}) copy-start(bf16[768,256]{1,0:T(8,128)(2,1)} %constant.25.clone.refs_3_) | copy-start | bytes 1179652
  2.9 51.0 %copy-start.5 = (bf16[768,256]{1,0:T(8,128)(2,1)S(1)}, bf16[768,256]{1,0:T(8,128)(2,1)}, u32[]{:S(2)}) copy-start(bf16[768,256]{1,0:T(8,128)(2,1)} %constant.26.clone.refs_4_) | copy-start | bytes 1179652
  2.9 50.9 %copy-start.6 = (bf16[256,384]{1,0:T(8,128)(2,1)S(1)}, bf16[256,384]{1,0:T(8,128)(2,1)}, u32[]{:S(2)}) copy-start(bf16[256,384]{1,0:T(8,128)(2,1)} %constant.23.clone.refs_1_) | copy-start | bytes 589828
  3.0 50.9 %copy-start.7 = (bf16[128,768]{1,0:T(8,128)(2,1)S(1)}, bf16[128,768]{1,0:T(8,128)(2,1)}, u32[]{:S(2)}) copy-start(bf16[128,768]{1,0:T(8,128)(2,1)} %constant.27.clone.refs_5_) | copy-start | bytes 589828
  3.0 50.9 %copy-start.8 = (bf16[256,192]{1,0:T(8,128)(2,1)S(1)}, bf16[256,192]{1,0:T(8,128)(2,1)}, u32[]{:S(2)}) copy-start(bf16[256,192]{1,0:T(8,128)(2,1)} %constant.24.clone.refs_2_) | copy-start | bytes 294916
  3.0 50.9 %copy-start.9 = (f32[128,256]{1,0:T(8,128)S(1)}, f32[128,256]{1,0:T(8,128)}, u32[]{:S(2)}) copy-start(f32[128,256]{1,0:T(8,128)} %constant.29.clone.refs_7_) | copy-start | bytes 393220
  3.0 50.9 %copy-start.10 = (bf16[64,768]{1,0:T(8,128)(2,1)S(1)}, bf16[64,768]{1,0:T(8,128)(2,1)}, u32[]{:S(2)}) copy-start(bf16[64,768]{1,0:T(8,128)(2,1)} %constant.28.clone.refs_6_) | copy-start | bytes 294916
  57.4 40.0 %copy-start.11 = (f32[512]{0:T(512)S(1)}, f32[512]{0:T(512)}, u32[]{:S(2)}) copy-start(f32[512]{0:T(512)} %param.17) | copy-start | bytes 6148
  57.5 40.2 %copy-start = (bf16[2,512,128]{2,1,0:T(8,128)(2,1)S(1)}, bf16[2,512,128]{2,1,0:T(8,128)(2,1)}, u32[]{:S(2)}) copy-start(bf16[2,512,128]{2,1,0:T(8,128)(2,1)} %refs_2_.4) | copy-start | bytes 786436
  57.5 40.2 %copy-start.1 = (bf16[2,512,128]{2,1,0:T(8,128)(2,1)S(1)}, bf16[2,512,128]{2,1,0:T(8,128)(2,1)}, u32[]{:S(2)}) copy-start(bf16[2,512,128]{2,1,0:T(8,128)(2,1)} %refs_3_.4) | copy-start | bytes 786436
  57.5 40.2 %copy-start.2 = (bf16[2,512,128]{2,1,0:T(8,128)(2,1)S(1)}, bf16[2,512,128]{2,1,0:T(8,128)(2,1)}, u32[]{:S(2)}) copy-start(bf16[2,512,128]{2,1,0:T(8,128)(2,1)} %refs_4_.4) | copy-start | bytes 786436
  57.5 40.2 %copy-start.3 = (bf16[2,512,128]{2,1,0:T(8,128)(2,1)S(1)}, bf16[2,512,128]{2,1,0:T(8,128)(2,1)}, u32[]{:S(2)}) copy-start(bf16[2,512,128]{2,1,0:T(8,128)(2,1)} %refs_5_.4) | copy-start | bytes 786436
  97.3 1.6 %collective-permute-start = (f32[256,128]{1,0:T(8,128)S(1)}, f32[256,128]{1,0:T(8,128)S(1)}, u32[]{:S(2)}, u32[]{:S(2)}) collective-permute-start(f32[256,128]{1,0:T(8,128)S(1)} %bitcast.12), channel_id=1, source_target_pairs={{0,1},{1,0},{2,3},{3,2},{4,5},{5,4},{6,7},{7,6},{8,9},{9,8},{10,11... | collective-permute-start | bytes 393224 | tf_op jit(solution)/shard_map/swap/ppermute | solution.py:304

commit v4 on v3

--- a/solution.py
+++ b/solution.py
@@ -111,9 +111,10 @@
                     at = base + (sig * batch + b) * own + j
                     send[pl.ds(at, peers, stride=rows), :] = slot[pl.ds(j, peers, stride=own), :]
         copies[5 * n + 4].wait()
-        send[pl.ds(base + 2 * batch * own, peers, stride=rows), :] = f[
-            pl.ds(n * span + core_ref[0], peers, stride=own), :
-        ]
+        row = f[pl.ds(n * span, peers, stride=own), :]
+        for j in range(1, own):
+            row = jnp.where(core_ref[0] == j, f[pl.ds(n * span + j, peers, stride=own), :], row)
+        send[pl.ds(base + 2 * batch * own, peers, stride=rows), :] = row
         block = pl.ds(base, peers * rows)
         sent.append(pltpu.make_async_copy(send.at[block], send_hbm.at[block], out_sems.at[n]))
         sent[n].start()
@@ -165,13 +166,13 @@
         r_ref[pl.ds(j * rows_in + 2 * batch * own, devices, stride=step_in), :]
         for j in range(own)
     ]
-    real = mm(enter_real[...], parts(jnp.concatenate(taps, 1), 0))
-    taps_spec = forward(real, own)
     loaded = [
         jnp.concatenate([load(j, sig, d) for sig in range(2) for d in range(groups)], 1)
         for j in range(own)
     ]
     entered = [mm(enter[...], parts(value, 0)) for value in loaded]
+    real = mm(enter_real[...], parts(jnp.concatenate(taps, 1), 0))
+    taps_spec = forward(real, own)
     specs = [forward(value, count) for value in entered]
     spreads, crosses = [], []
     for j in range(own):
@@ -241,9 +242,10 @@
 
 def join_kernel(own, core_ref, mine_ref, other_ref, out_ref):
     peers = mine_ref.shape[0]
-    core = core_ref[0]
-    out_ref[pl.ds(core, peers, stride=own), :] = mine_ref[...]
-    out_ref[pl.ds(own - 1 - core, peers, stride=own), :] = other_ref[...]
+    for j in range(own):
+        out_ref[pl.ds(j, peers, stride=own), :] = jnp.where(
+            core_ref[0] == j, mine_ref[...], other_ref[...]
+        )
 
 
 VMEM = pl.BlockSpec(memory_space=pltpu.VMEM)

time: 99.9 us -> 99.8 us (level)
  no operation moved by 1% of the time
where the time goes in v4:
time: 99.8 us; the launch traced here: 99.6 us
  blocking collectives  90.6 us (91%)
  Pallas kernels  7.73 us (8%)
    all_to_all x1, blocking collectives, exchange(): lax.all_to_all(shaped, ('seq', 'dp'), split_axis=0, concat_axis=0, tiled=...  50.9 us
    all_to_all x1, blocking collectives, shards(): lax.all_to_all(shaped, ('seq', 'dp'), split_axis=0, concat_axis=0, tiled=...  39.7 us
    pallas_call x1, Pallas kernels, shards(): pl.pallas_call(lambda *refs: mid_kernel(devices, groups, own, batch, rows...  3.48 us
    pallas_call x1, Pallas kernels, shards(): pl.pallas_call(lambda *refs: pre_kernel(rows_in, own, *refs), out_shape=j...  2.27 us
  transfers between devices with their start and end apart: 1, of which 0 were waited for; matrix products, arithmetic and copies ran while one was open for 0% of the time, Pallas kernels for 1%

profile of v4, /device:TPU:1, one launch (start us, length us, event | category | flops | bytes accessed | tf_op | source)
XLA Modules:
  0.0 99.6 jit_solution(14398203059363071218)
XLA Ops:
  0.6 2.3 %pre.1 = f32[2304,128]{1,0:T(8,128)} custom-call(s32[1]{0:T(128)} %bitcast.refs_0_, bf16[2,512,128]{2,1,0:T(8,128)(2,1)} %refs_2_.4, bf16[2,512,128]{2,1,0:T(8,128)(2,1)} %refs_3_.4, bf16[2,512,128]{2,1,0:T(8,128)(2,1)} %refs_4_.4, bf16[2,512,128]{2,1,0:T(8,128)(2,1)} %refs_5_.4, f32[512,128]{1,0:T(8,128)} %refs_5_.3), custom_call_target="tpu_custom_call" | custom-call | tf_op jit(solution)/shard_map/pre/pallas_call | solution.py:275
  2.9 0.0 copy-start.4
  2.9 0.0 copy-start.5
  2.9 0.0 copy-start.6
  3.0 0.0 copy-start.7
  3.0 0.0 copy-start.8
  3.0 0.0 copy-start.9
  3.0 0.0 copy-start.10
  3.0 50.9 %all_to_all.10 = f32[256,9,1,128]{3,2,1,0:T(1,128)S(1)} all-to-all(f32[256,9,1,128]{3,2,1,0:T(1,128)} %bitcast.14), channel_id=1, replica_groups=mesh['seq'=64,'dp'=4] {'seq','dp'}, dimensions={0} | all-to-all | bytes 2359296 | tf_op jit(solution)/shard_map/gather/all_to_all | solution.py:270
  53.9 0.0 copy-done.4
  53.9 0.0 copy-done.5
  53.9 0.0 copy-done.6
  53.9 0.0 copy-done.7
  53.9 0.0 copy-done.8
  53.9 0.0 copy-done.9
  53.9 0.0 copy-done.10
  53.9 3.5 %mid.1 = f32[2304,128]{1,0:T(8,128)S(1)} custom-call(f32[2304,128]{1,0:T(8,128)S(1)} %bitcast.10, bf16[256,384]{1,0:T(8,128)(2,1)S(1)} %copy-done.6, bf16[256,192]{1,0:T(8,128)(2,1)S(1)} %copy-done.8, bf16[768,256]{1,0:T(8,128)(2,1)S(1)} %copy-done.4, bf16[768,256]{1,0:T(8,128)(2,1)S(1)} %copy-done.5, bf16[128,768]{1,0:T(8,128)(2,1)S(1)} %copy-done.7, ...), custom_call_target="tpu_custom_call" | custom-call | tf_op jit(solution)/shard_map/mid/pallas_call | solution.py:293
  57.4 0.0 copy-start.11
  57.4 0.0 copy-start
  57.4 0.0 copy-start.1
  57.4 0.0 copy-start.2
  57.5 0.0 copy-start.3
  57.5 39.7 %all_to_all.11 = f32[256,9,1,128]{3,2,1,0:T(1,128)S(1)} all-to-all(f32[256,9,1,128]{3,2,1,0:T(1,128)S(1)} %bitcast.11), channel_id=1, replica_groups=mesh['seq'=64,'dp'=4] {'seq','dp'}, dimensions={0} | all-to-all | bytes 2359296 | tf_op jit(solution)/shard_map/scatter/all_to_all | solution.py:302
  97.2 0.1 slice.4
  97.3 0.1 collective-permute-start
  97.4 0.0 copy-done.11
  97.4 0.1 copy.23.refs_1_
  97.6 0.0 copy-done
  97.6 0.0 copy-done.1
  97.6 0.0 copy-done.2
  97.6 0.0 copy-done.3
  97.6 1.2 %post.1 = (bf16[2,512,128]{2,1,0:T(8,128)(2,1)}, bf16[2,512,128]{2,1,0:T(8,128)(2,1)}, bf16[2,512,128]{2,1,0:T(8,128)(2,1)}, bf16[2,512,128]{2,1,0:T(8,128)(2,1)}) custom-call(f32[2304,128]{1,0:T(8,128)S(1)} %bitcast.9, f32[512,1]{1,0:T(8,128)S(1)} %copy.23.refs_1_, bf16[2,512,128]{2,1,0:T(8,128)(2,1)S(1)} %copy-done, bf16[2,512,128]{2,1,0:T(8,128)(2,1)S(1)} %copy-done.1, ...), custom_call_target="tpu_custom_call" | custom-call | flops 1000000 | bytes 4000000 | tf_op jit(solution)/shard_map/post/pallas_call | solution.py:309
  98.9 0.0 collective-permute-done.refs_2_
  98.9 0.7 join.1
Async XLA Ops:
  2.9 51.0 %copy-start.4 = (bf16[768,256]{1,0:T(8,128)(2,1)S(1)}, bf16[768,256]{1,0:T(8,128)(2,1)}, u32[]{:S(2)}) copy-start(bf16[768,256]{1,0:T(8,128)(2,1)} %constant.25.clone.refs_3_) | copy-start | bytes 1179652
  2.9 51.0 %copy-start.5 = (bf16[768,256]{1,0:T(8,128)(2,1)S(1)}, bf16[768,256]{1,0:T(8,128)(2,1)}, u32[]{:S(2)}) copy-start(bf16[768,256]{1,0:T(8,128)(2,1)} %constant.26.clone.refs_4_) | copy-start | bytes 1179652
  2.9 50.9 %copy-start.6 = (bf16[256,384]{1,0:T(8,128)(2,1)S(1)}, bf16[256,384]{1,0:T(8,128)(2,1)}, u32[]{:S(2)}) copy-start(bf16[256,384]{1,0:T(8,128)(2,1)} %constant.23.clone.refs_1_) | copy-start | bytes 589828
  3.0 50.9 %copy-start.7 = (bf16[128,768]{1,0:T(8,128)(2,1)S(1)}, bf16[128,768]{1,0:T(8,128)(2,1)}, u32[]{:S(2)}) copy-start(bf16[128,768]{1,0:T(8,128)(2,1)} %constant.27.clone.refs_5_) | copy-start | bytes 589828
  3.0 50.9 %copy-start.8 = (bf16[256,192]{1,0:T(8,128)(2,1)S(1)}, bf16[256,192]{1,0:T(8,128)(2,1)}, u32[]{:S(2)}) copy-start(bf16[256,192]{1,0:T(8,128)(2,1)} %constant.24.clone.refs_2_) | copy-start | bytes 294916
  3.0 50.9 %copy-start.9 = (f32[128,256]{1,0:T(8,128)S(1)}, f32[128,256]{1,0:T(8,128)}, u32[]{:S(2)}) copy-start(f32[128,256]{1,0:T(8,128)} %constant.29.clone.refs_7_) | copy-start | bytes 393220
  3.0 50.9 %copy-start.10 = (bf16[64,768]{1,0:T(8,128)(2,1)S(1)}, bf16[64,768]{1,0:T(8,128)(2,1)}, u32[]{:S(2)}) copy-start(bf16[64,768]{1,0:T(8,128)(2,1)} %constant.28.clone.refs_6_) | copy-start | bytes 294916
  57.4 40.0 %copy-start.11 = (f32[512]{0:T(512)S(1)}, f32[512]{0:T(512)}, u32[]{:S(2)}) copy-start(f32[512]{0:T(512)} %param.17) | copy-start | bytes 6148
  57.4 40.2 %copy-start = (bf16[2,512,128]{2,1,0:T(8,128)(2,1)S(1)}, bf16[2,512,128]{2,1,0:T(8,128)(2,1)}, u32[]{:S(2)}) copy-start(bf16[2,512,128]{2,1,0:T(8,128)(2,1)} %refs_2_.4) | copy-start | bytes 786436
  57.4 40.2 %copy-start.1 = (bf16[2,512,128]{2,1,0:T(8,128)(2,1)S(1)}, bf16[2,512,128]{2,1,0:T(8,128)(2,1)}, u32[]{:S(2)}) copy-start(bf16[2,512,128]{2,1,0:T(8,128)(2,1)} %refs_3_.4) | copy-start | bytes 786436
  57.4 40.1 %copy-start.2 = (bf16[2,512,128]{2,1,0:T(8,128)(2,1)S(1)}, bf16[2,512,128]{2,1,0:T(8,128)(2,1)}, u32[]{:S(2)}) copy-start(bf16[2,512,128]{2,1,0:T(8,128)(2,1)} %refs_4_.4) | copy-start | bytes 786436
  57.5 40.1 %copy-start.3 = (bf16[2,512,128]{2,1,0:T(8,128)(2,1)S(1)}, bf16[2,512,128]{2,1,0:T(8,128)(2,1)}, u32[]{:S(2)}) copy-start(bf16[2,512,128]{2,1,0:T(8,128)(2,1)} %refs_5_.4) | copy-start | bytes 786436
  97.3 1.6 %collective-permute-start = (f32[256,128]{1,0:T(8,128)S(1)}, f32[256,128]{1,0:T(8,128)S(1)}, u32[]{:S(2)}, u32[]{:S(2)}) collective-permute-start(f32[256,128]{1,0:T(8,128)S(1)} %bitcast.12), channel_id=1, source_target_pairs={{0,1},{1,0},{2,3},{3,2},{4,5},{5,4},{6,7},{7,6},{8,9},{9,8},{10,11... | collective-permute-start | bytes 393224 | tf_op jit(solution)/shard_map/swap/ppermute | solution.py:306

commit v5 on v4

--- a/solution.py
+++ b/solution.py
@@ -81,8 +81,7 @@
 
 
 def pre_kernel(
-    rows, own, core_ref, q_hbm, k_hbm, v_hbm, g_hbm, f_hbm, send_hbm, q, k, v, g, f, send, hold,
-    sems, out_sems,
+    rows, own, core_ref, q_hbm, k_hbm, v_hbm, g_hbm, f_hbm, send, q, k, v, g, f, hold, sems
 ):
     batch, chans = q.shape[0], q.shape[1]
     span = chans // CHUNKS
@@ -97,7 +96,6 @@
         copies.append(pltpu.make_async_copy(f_hbm.at[part], f.at[part], sems.at[5 * n + 4]))
     for copy in copies:
         copy.start()
-    sent = []
     for n in range(CHUNKS):
         part = pl.ds(n * span, span)
         base = n * peers * rows
@@ -115,11 +113,6 @@
         for j in range(1, own):
             row = jnp.where(core_ref[0] == j, f[pl.ds(n * span + j, peers, stride=own), :], row)
         send[pl.ds(base + 2 * batch * own, peers, stride=rows), :] = row
-        block = pl.ds(base, peers * rows)
-        sent.append(pltpu.make_async_copy(send.at[block], send_hbm.at[block], out_sems.at[n]))
-        sent[n].start()
-    for copy in sent:
-        copy.wait()
 
 
 def leave_product(table, data):
@@ -274,18 +267,16 @@
         wide = pltpu.VMEM((batch, chans, cols), BF16)
         send = pl.pallas_call(
             lambda *refs: pre_kernel(rows_in, own, *refs),
-            out_shape=jax.ShapeDtypeStruct((peers * rows_in, cols), F32),
+            out_shape=pltpu.VMEM((peers * rows_in, cols), F32),
             in_specs=[SMEM] + [HBM] * 5,
-            out_specs=HBM,
+            out_specs=VMEM,
             scratch_shapes=[
                 wide, wide, wide, wide,
                 pltpu.VMEM((chans, cols), F32),
-                pltpu.VMEM((peers * rows_in, cols), F32),
                 pltpu.VMEM((2 * batch * CHUNKS, chans // CHUNKS, cols), F32),
                 pltpu.SemaphoreType.DMA((5 * CHUNKS,)),
-                pltpu.SemaphoreType.DMA((CHUNKS,)),
             ],
-            compiler_params=params(62),
+            compiler_params=params(56),
         )(core, query_proj, key_proj, value_proj, out_grad, long_filter)
     with jax.named_scope("gather"):
         arrived = exchange(send, rows_in)

time: 99.8 us -> 98.9 us (level)
  no operation moved by 1% of the time
where the time goes in v5:
time: 98.9 us; the launch traced here: 98.6 us
  blocking collectives  90.4 us (91%)
  Pallas kernels  6.98 us (7%)
    all_to_all x1, blocking collectives, exchange(): lax.all_to_all(shaped, ('seq', 'dp'), split_axis=0, concat_axis=0, tiled=...  50.7 us
    all_to_all x1, blocking collectives, shards(): lax.all_to_all(shaped, ('seq', 'dp'), split_axis=0, concat_axis=0, tiled=...  39.7 us
    pallas_call x1, Pallas kernels, shards(): pl.pallas_call(lambda *refs: mid_kernel(devices, groups, own, batch, rows...  3.49 us
  transfers between devices with their start and end apart: 1, of which 0 were waited for; matrix products, arithmetic and copies ran while one was open for 0% of the time, Pallas kernels for 1%

profile of v5, /device:TPU:1, one launch (start us, length us, event | category | flops | bytes accessed | tf_op | source)
XLA Modules:
  0.0 98.6 jit_solution(4912819341910165971)
XLA Ops:
  0.6 1.5 %pre.1 = f32[2304,128]{1,0:T(8,128)S(1)} custom-call(s32[1]{0:T(128)} %bitcast.refs_0_, bf16[2,512,128]{2,1,0:T(8,128)(2,1)} %refs_2_.4, bf16[2,512,128]{2,1,0:T(8,128)(2,1)} %refs_3_.4, bf16[2,512,128]{2,1,0:T(8,128)(2,1)} %refs_4_.4, bf16[2,512,128]{2,1,0:T(8,128)(2,1)} %refs_5_.4, f32[512,128]{1,0:T(8,128)} %refs_5_.3), custom_call_target="tpu_custom_call" | custom-call | tf_op jit(solution)/shard_map/pre/pallas_call | solution.py:268
  2.2 0.0 copy-start.4
  2.2 0.0 copy-start.5
  2.2 0.0 copy-start.6
  2.2 0.0 copy-start.7
  2.2 0.0 copy-start.8
  2.2 0.0 copy-start.9
  2.2 0.0 copy-start.10
  2.3 50.7 %all_to_all.10 = f32[256,9,1,128]{3,2,1,0:T(1,128)S(1)} all-to-all(f32[256,9,1,128]{3,2,1,0:T(1,128)S(1)} %bitcast.10), channel_id=1, replica_groups=mesh['seq'=64,'dp'=4] {'seq','dp'}, dimensions={0} | all-to-all | bytes 2359296 | tf_op jit(solution)/shard_map/gather/all_to_all | solution.py:263
  52.9 0.0 copy-done.4
  52.9 0.0 copy-done.5
  52.9 0.0 copy-done.6
  52.9 0.0 copy-done.7
  52.9 0.0 copy-done.8
  52.9 0.0 copy-done.9
  53.0 0.0 copy-done.10
  53.0 3.5 %mid.1 = f32[2304,128]{1,0:T(8,128)S(1)} custom-call(f32[2304,128]{1,0:T(8,128)S(1)} %bitcast.11, bf16[256,384]{1,0:T(8,128)(2,1)S(1)} %copy-done.6, bf16[256,192]{1,0:T(8,128)(2,1)S(1)} %copy-done.8, bf16[768,256]{1,0:T(8,128)(2,1)S(1)} %copy-done.4, bf16[768,256]{1,0:T(8,128)(2,1)S(1)} %copy-done.5, bf16[128,768]{1,0:T(8,128)(2,1)S(1)} %copy-done.7, ...), custom_call_target="tpu_custom_call" | custom-call | tf_op jit(solution)/shard_map/mid/pallas_call | solution.py:284
  56.4 0.0 copy-start.11
  56.5 0.0 copy-start
  56.5 0.0 copy-start.1
  56.5 0.0 copy-start.2
  56.5 0.0 copy-start.3
  56.5 39.7 %all_to_all.11 = f32[256,9,1,128]{3,2,1,0:T(1,128)S(1)} all-to-all(f32[256,9,1,128]{3,2,1,0:T(1,128)S(1)} %bitcast.12), channel_id=1, replica_groups=mesh['seq'=64,'dp'=4] {'seq','dp'}, dimensions={0} | all-to-all | bytes 2359296 | tf_op jit(solution)/shard_map/scatter/all_to_all | solution.py:293
  96.3 0.1 slice.4
  96.3 0.1 collective-permute-start
  96.4 0.0 copy-done.11
  96.5 0.1 copy.23.refs_1_
  96.6 0.0 copy-done
  96.6 0.0 copy-done.1
  96.6 0.0 copy-done.2
  96.6 0.0 copy-done.3
  96.6 1.2 %post.1 = (bf16[2,512,128]{2,1,0:T(8,128)(2,1)}, bf16[2,512,128]{2,1,0:T(8,128)(2,1)}, bf16[2,512,128]{2,1,0:T(8,128)(2,1)}, bf16[2,512,128]{2,1,0:T(8,128)(2,1)}) custom-call(f32[2304,128]{1,0:T(8,128)S(1)} %bitcast.9, f32[512,1]{1,0:T(8,128)S(1)} %copy.23.refs_1_, bf16[2,512,128]{2,1,0:T(8,128)(2,1)S(1)} %copy-done, bf16[2,512,128]{2,1,0:T(8,128)(2,1)S(1)} %copy-done.1, ...), custom_call_target="tpu_custom_call" | custom-call | flops 1000000 | bytes 4000000 | tf_op jit(solution)/shard_map/post/pallas_call | solution.py:300
  97.9 0.0 collective-permute-done.refs_2_
  97.9 0.7 join.1
Async XLA Ops:
  2.2 50.7 %copy-start.4 = (bf16[768,256]{1,0:T(8,128)(2,1)S(1)}, bf16[768,256]{1,0:T(8,128)(2,1)}, u32[]{:S(2)}) copy-start(bf16[768,256]{1,0:T(8,128)(2,1)} %constant.25.clone.refs_3_) | copy-start | bytes 1179652
  2.2 50.7 %copy-start.5 = (bf16[768,256]{1,0:T(8,128)(2,1)S(1)}, bf16[768,256]{1,0:T(8,128)(2,1)}, u32[]{:S(2)}) copy-start(bf16[768,256]{1,0:T(8,128)(2,1)} %constant.26.clone.refs_4_) | copy-start | bytes 1179652
  2.2 50.7 %copy-start.6 = (bf16[256,384]{1,0:T(8,128)(2,1)S(1)}, bf16[256,384]{1,0:T(8,128)(2,1)}, u32[]{:S(2)}) copy-start(bf16[256,384]{1,0:T(8,128)(2,1)} %constant.23.clone.refs_1_) | copy-start | bytes 589828
  2.2 50.7 %copy-start.7 = (bf16[128,768]{1,0:T(8,128)(2,1)S(1)}, bf16[128,768]{1,0:T(8,128)(2,1)}, u32[]{:S(2)}) copy-start(bf16[128,768]{1,0:T(8,128)(2,1)} %constant.27.clone.refs_5_) | copy-start | bytes 589828
  2.2 50.7 %copy-start.8 = (bf16[256,192]{1,0:T(8,128)(2,1)S(1)}, bf16[256,192]{1,0:T(8,128)(2,1)}, u32[]{:S(2)}) copy-start(bf16[256,192]{1,0:T(8,128)(2,1)} %constant.24.clone.refs_2_) | copy-start | bytes 294916
  2.2 50.7 %copy-start.9 = (f32[128,256]{1,0:T(8,128)S(1)}, f32[128,256]{1,0:T(8,128)}, u32[]{:S(2)}) copy-start(f32[128,256]{1,0:T(8,128)} %constant.29.clone.refs_7_) | copy-start | bytes 393220
  2.2 50.7 %copy-start.10 = (bf16[64,768]{1,0:T(8,128)(2,1)S(1)}, bf16[64,768]{1,0:T(8,128)(2,1)}, u32[]{:S(2)}) copy-start(bf16[64,768]{1,0:T(8,128)(2,1)} %constant.28.clone.refs_6_) | copy-start | bytes 294916
  56.4 40.0 %copy-start.11 = (f32[512]{0:T(512)S(1)}, f32[512]{0:T(512)}, u32[]{:S(2)}) copy-start(f32[512]{0:T(512)} %param.17) | copy-start | bytes 6148
  56.5 40.2 %copy-start = (bf16[2,512,128]{2,1,0:T(8,128)(2,1)S(1)}, bf16[2,512,128]{2,1,0:T(8,128)(2,1)}, u32[]{:S(2)}) copy-start(bf16[2,512,128]{2,1,0:T(8,128)(2,1)} %refs_2_.4) | copy-start | bytes 786436
  56.5 40.1 %copy-start.1 = (bf16[2,512,128]{2,1,0:T(8,128)(2,1)S(1)}, bf16[2,512,128]{2,1,0:T(8,128)(2,1)}, u32[]{:S(2)}) copy-start(bf16[2,512,128]{2,1,0:T(8,128)(2,1)} %refs_3_.4) | copy-start | bytes 786436
  56.5 40.1 %copy-start.2 = (bf16[2,512,128]{2,1,0:T(8,128)(2,1)S(1)}, bf16[2,512,128]{2,1,0:T(8,128)(2,1)}, u32[]{:S(2)}) copy-start(bf16[2,512,128]{2,1,0:T(8,128)(2,1)} %refs_4_.4) | copy-start | bytes 786436
  56.5 40.1 %copy-start.3 = (bf16[2,512,128]{2,1,0:T(8,128)(2,1)S(1)}, bf16[2,512,128]{2,1,0:T(8,128)(2,1)}, u32[]{:S(2)}) copy-start(bf16[2,512,128]{2,1,0:T(8,128)(2,1)} %refs_5_.4) | copy-start | bytes 786436
  96.3 1.6 %collective-permute-start = (f32[256,128]{1,0:T(8,128)S(1)}, f32[256,128]{1,0:T(8,128)S(1)}, u32[]{:S(2)}, u32[]{:S(2)}) collective-permute-start(f32[256,128]{1,0:T(8,128)S(1)} %bitcast.13), channel_id=1, source_target_pairs={{0,1},{1,0},{2,3},{3,2},{4,5},{5,4},{6,7},{7,6},{8,9},{9,8},{10,11... | collective-permute-start | bytes 393224 | tf_op jit(solution)/shard_map/swap/ppermute | solution.py:297

commit v6 on v5

--- a/solution.py
+++ b/solution.py
@@ -84,35 +84,28 @@
     rows, own, core_ref, q_hbm, k_hbm, v_hbm, g_hbm, f_hbm, send, q, k, v, g, f, hold, sems
 ):
     batch, chans = q.shape[0], q.shape[1]
-    span = chans // CHUNKS
-    peers = span // own
-    copies = []
-    for n in range(CHUNKS):
-        part = pl.ds(n * span, span)
-        for i, (src, dst) in enumerate(((k_hbm, k), (v_hbm, v), (g_hbm, g), (q_hbm, q))):
-            copies.append(
-                pltpu.make_async_copy(src.at[:, part], dst.at[:, part], sems.at[5 * n + i])
-            )
-        copies.append(pltpu.make_async_copy(f_hbm.at[part], f.at[part], sems.at[5 * n + 4]))
+    peers = chans // own
+    planes = ((k_hbm, k), (v_hbm, v), (g_hbm, g), (q_hbm, q), (f_hbm, f))
+    copies = [
+        pltpu.make_async_copy(src, dst, sems.at[i]) for i, (src, dst) in enumerate(planes)
+    ]
     for copy in copies:
         copy.start()
-    for n in range(CHUNKS):
-        part = pl.ds(n * span, span)
-        base = n * peers * rows
-        for sig, (left, right) in enumerate(((k, v), (g, q))):
-            copies[5 * n + 2 * sig].wait()
-            copies[5 * n + 2 * sig + 1].wait()
-            for b in range(batch):
-                slot = hold.at[(2 * n + sig) * batch + b]
-                slot[...] = left[b, part].astype(F32) * right[b, part].astype(F32)
-                for j in range(own):
-                    at = base + (sig * batch + b) * own + j
-                    send[pl.ds(at, peers, stride=rows), :] = slot[pl.ds(j, peers, stride=own), :]
-        copies[5 * n + 4].wait()
-        row = f[pl.ds(n * span, peers, stride=own), :]
-        for j in range(1, own):
-            row = jnp.where(core_ref[0] == j, f[pl.ds(n * span + j, peers, stride=own), :], row)
-        send[pl.ds(base + 2 * batch * own, peers, stride=rows), :] = row
+    for sig, (left, right) in enumerate(((k, v), (g, q))):
+        copies[2 * sig].wait()
+        copies[2 * sig + 1].wait()
+        for b in range(batch):
+            slot = hold.at[sig * batch + b]
+            slot[...] = left[b].astype(F32) * right[b].astype(F32)
+            for j in range(own):
+                send[pl.ds((sig * batch + b) * own + j, peers, stride=rows), :] = slot[
+                    pl.ds(j, peers, stride=own), :
+                ]
+    copies[4].wait()
+    row = f[pl.ds(0, peers, stride=own), :]
+    for j in range(1, own):
+        row = jnp.where(core_ref[0] == j, f[pl.ds(j, peers, stride=own), :], row)
+    send[pl.ds(2 * batch * own, peers, stride=rows), :] = row
 
 
 def leave_product(table, data):
@@ -209,7 +202,7 @@
     sent = []
     for n in range(CHUNKS):
         part = pl.ds(n * span, span)
-        skip = skip_ref[part, :]
+        skip = jnp.broadcast_to(skip_ref[n : n + 1, :], (LANES, span)).T
         for b in range(batch):
             conv, back = conv_ref.at[n * batch + b], back_ref.at[n * batch + b]
             for j in range(own):
@@ -273,8 +266,8 @@
             scratch_shapes=[
                 wide, wide, wide, wide,
                 pltpu.VMEM((chans, cols), F32),
-                pltpu.VMEM((2 * batch * CHUNKS, chans // CHUNKS, cols), F32),
-                pltpu.SemaphoreType.DMA((5 * CHUNKS,)),
+                pltpu.VMEM((2 * batch, chans, cols), F32),
+                pltpu.SemaphoreType.DMA((5,)),
             ],
             compiler_params=params(56),
         )(core, query_proj, key_proj, value_proj, out_grad, long_filter)
@@ -307,7 +300,7 @@
             + [pltpu.SemaphoreType.DMA((4 * CHUNKS,))],
             compiler_params=params(48),
             cost_estimate=pl.CostEstimate(flops=10**6, bytes_accessed=4 * 10**6, transcendentals=0),
-        )(returned.reshape(peers * rows_out, cols), skip_gain[:, None], query_proj, key_proj, value_proj, out_grad)
+        )(returned.reshape(peers * rows_out, cols), skip_gain.reshape(CHUNKS, chans // CHUNKS), query_proj, key_proj, value_proj, out_grad)
     with jax.named_scope("join"):
         grad_filter = pl.pallas_call(
             lambda *refs: join_kernel(own, *refs),

time: 98.9 us -> 98.6 us (level)
  no operation moved by 1% of the time
where the time goes in v6:
time: 98.6 us; the launch traced here: 98.4 us
  blocking collectives  90.4 us (92%)
  Pallas kernels  6.91 us (7%)
    all_to_all x1, blocking collectives, exchange(): lax.all_to_all(shaped, ('seq', 'dp'), split_axis=0, concat_axis=0, tiled=...  50.7 us
    all_to_all x1, blocking collectives, shards(): lax.all_to_all(shaped, ('seq', 'dp'), split_axis=0, concat_axis=0, tiled=...  39.7 us
    pallas_call x1, Pallas kernels, shards(): pl.pallas_call(lambda *refs: mid_kernel(devices, groups, own, batch, rows...  3.49 us
  transfers between devices with their start and end apart: 1, of which 0 were waited for; matrix products, arithmetic and copies ran while one was open for 0% of the time, Pallas kernels for 1%

profile of v6, /device:TPU:1, one launch (start us, length us, event | category | flops | bytes accessed | tf_op | source)
XLA Modules:
  0.0 98.4 jit_solution(2983814645133325638)
XLA Ops:
  0.6 1.4 %pre.1 = f32[2304,128]{1,0:T(8,128)S(1)} custom-call(s32[1]{0:T(128)} %bitcast.refs_0_, bf16[2,512,128]{2,1,0:T(8,128)(2,1)} %refs_2_.4, bf16[2,512,128]{2,1,0:T(8,128)(2,1)} %refs_3_.4, bf16[2,512,128]{2,1,0:T(8,128)(2,1)} %refs_4_.4, bf16[2,512,128]{2,1,0:T(8,128)(2,1)} %refs_5_.4, f32[512,128]{1,0:T(8,128)} %refs_5_.3), custom_call_target="tpu_custom_call" | custom-call | tf_op jit(solution)/shard_map/pre/pallas_call | solution.py:261
  2.0 0.0 copy-start.4
  2.0 0.0 copy-start.5
  2.0 0.0 copy-start.6
  2.0 0.0 copy-start.7
  2.1 0.0 copy-start.8
  2.1 0.0 copy-start.9
  2.1 0.0 copy-start.10
  2.1 50.7 %all_to_all.10 = f32[256,9,1,128]{3,2,1,0:T(1,128)S(1)} all-to-all(f32[256,9,1,128]{3,2,1,0:T(1,128)S(1)} %bitcast.10), channel_id=1, replica_groups=mesh['seq'=64,'dp'=4] {'seq','dp'}, dimensions={0} | all-to-all | bytes 2359296 | tf_op jit(solution)/shard_map/gather/all_to_all | solution.py:256
  52.8 0.0 copy-done.4
  52.8 0.0 copy-done.5
  52.8 0.0 copy-done.6
  52.8 0.0 copy-done.7
  52.8 0.0 copy-done.8
  52.8 0.0 copy-done.9
  52.8 0.0 copy-done.10
  52.8 3.5 %mid.1 = f32[2304,128]{1,0:T(8,128)S(1)} custom-call(f32[2304,128]{1,0:T(8,128)S(1)} %bitcast.11, bf16[256,384]{1,0:T(8,128)(2,1)S(1)} %copy-done.6, bf16[256,192]{1,0:T(8,128)(2,1)S(1)} %copy-done.8, bf16[768,256]{1,0:T(8,128)(2,1)S(1)} %copy-done.4, bf16[768,256]{1,0:T(8,128)(2,1)S(1)} %copy-done.5, bf16[128,768]{1,0:T(8,128)(2,1)S(1)} %copy-done.7, ...), custom_call_target="tpu_custom_call" | custom-call | tf_op jit(solution)/shard_map/mid/pallas_call | solution.py:277
  56.3 0.0 copy-start
  56.3 0.0 copy-start.1
  56.3 0.0 copy-start.2
  56.3 0.0 copy-start.3
  56.3 0.0 copy-start.11
  56.4 39.7 %all_to_all.11 = f32[256,9,1,128]{3,2,1,0:T(1,128)S(1)} all-to-all(f32[256,9,1,128]{3,2,1,0:T(1,128)S(1)} %bitcast.12), channel_id=1, replica_groups=mesh['seq'=64,'dp'=4] {'seq','dp'}, dimensions={0} | all-to-all | bytes 2359296 | tf_op jit(solution)/shard_map/scatter/all_to_all | solution.py:286
  96.1 0.1 slice.4
  96.2 0.1 collective-permute-start
  96.3 0.0 copy-done
  96.3 0.0 copy-done.1
  96.3 0.0 copy-done.2
  96.3 0.0 copy-done.3
  96.3 0.0 copy-done.11
  96.3 1.3 %post.1 = (bf16[2,512,128]{2,1,0:T(8,128)(2,1)}, bf16[2,512,128]{2,1,0:T(8,128)(2,1)}, bf16[2,512,128]{2,1,0:T(8,128)(2,1)}, bf16[2,512,128]{2,1,0:T(8,128)(2,1)}) custom-call(f32[2304,128]{1,0:T(8,128)S(1)} %bitcast.9, f32[4,128]{1,0:T(4,128)S(1)} %bitcast.15, bf16[2,512,128]{2,1,0:T(8,128)(2,1)S(1)} %copy-done, bf16[2,512,128]{2,1,0:T(8,128)(2,1)S(1)} %copy-done.1, ...), custom_call_target="tpu_custom_call" | custom-call | flops 1000000 | bytes 4000000 | tf_op jit(solution)/shard_map/post/pallas_call | solution.py:293
  97.7 0.0 collective-permute-done.refs_2_
  97.7 0.7 join.1
Async XLA Ops:
  2.0 50.7 %copy-start.4 = (bf16[768,256]{1,0:T(8,128)(2,1)S(1)}, bf16[768,256]{1,0:T(8,128)(2,1)}, u32[]{:S(2)}) copy-start(bf16[768,256]{1,0:T(8,128)(2,1)} %constant.25.clone.refs_3_) | copy-start | bytes 1179652
  2.0 50.7 %copy-start.5 = (bf16[768,256]{1,0:T(8,128)(2,1)S(1)}, bf16[768,256]{1,0:T(8,128)(2,1)}, u32[]{:S(2)}) copy-start(bf16[768,256]{1,0:T(8,128)(2,1)} %constant.26.clone.refs_4_) | copy-start | bytes 1179652
  2.0 50.7 %copy-start.6 = (bf16[256,384]{1,0:T(8,128)(2,1)S(1)}, bf16[256,384]{1,0:T(8,128)(2,1)}, u32[]{:S(2)}) copy-start(bf16[256,384]{1,0:T(8,128)(2,1)} %constant.23.clone.refs_1_) | copy-start | bytes 589828
  2.0 50.7 %copy-start.7 = (bf16[128,768]{1,0:T(8,128)(2,1)S(1)}, bf16[128,768]{1,0:T(8,128)(2,1)}, u32[]{:S(2)}) copy-start(bf16[128,768]{1,0:T(8,128)(2,1)} %constant.27.clone.refs_5_) | copy-start | bytes 589828
  2.1 50.7 %copy-start.8 = (bf16[256,192]{1,0:T(8,128)(2,1)S(1)}, bf16[256,192]{1,0:T(8,128)(2,1)}, u32[]{:S(2)}) copy-start(bf16[256,192]{1,0:T(8,128)(2,1)} %constant.24.clone.refs_2_) | copy-start | bytes 294916
  2.1 50.7 %copy-start.9 = (f32[128,256]{1,0:T(8,128)S(1)}, f32[128,256]{1,0:T(8,128)}, u32[]{:S(2)}) copy-start(f32[128,256]{1,0:T(8,128)} %constant.29.clone.refs_7_) | copy-start | bytes 393220
  2.1 50.7 %copy-start.10 = (bf16[64,768]{1,0:T(8,128)(2,1)S(1)}, bf16[64,768]{1,0:T(8,128)(2,1)}, u32[]{:S(2)}) copy-start(bf16[64,768]{1,0:T(8,128)(2,1)} %constant.28.clone.refs_6_) | copy-start | bytes 294916
  56.3 40.0 %copy-start = (bf16[2,512,128]{2,1,0:T(8,128)(2,1)S(1)}, bf16[2,512,128]{2,1,0:T(8,128)(2,1)}, u32[]{:S(2)}) copy-start(bf16[2,512,128]{2,1,0:T(8,128)(2,1)} %refs_2_.4) | copy-start | bytes 786436
  56.3 40.0 %copy-start.1 = (bf16[2,512,128]{2,1,0:T(8,128)(2,1)S(1)}, bf16[2,512,128]{2,1,0:T(8,128)(2,1)}, u32[]{:S(2)}) copy-start(bf16[2,512,128]{2,1,0:T(8,128)(2,1)} %refs_3_.4) | copy-start | bytes 786436
  56.3 40.0 %copy-start.2 = (bf16[2,512,128]{2,1,0:T(8,128)(2,1)S(1)}, bf16[2,512,128]{2,1,0:T(8,128)(2,1)}, u32[]{:S(2)}) copy-start(bf16[2,512,128]{2,1,0:T(8,128)(2,1)} %refs_4_.4) | copy-start | bytes 786436
  56.3 40.0 %copy-start.3 = (bf16[2,512,128]{2,1,0:T(8,128)(2,1)S(1)}, bf16[2,512,128]{2,1,0:T(8,128)(2,1)}, u32[]{:S(2)}) copy-start(bf16[2,512,128]{2,1,0:T(8,128)(2,1)} %refs_5_.4) | copy-start | bytes 786436
  56.3 40.0 %copy-start.11 = (f32[512]{0:T(512)S(1)}, f32[512]{0:T(512)}, u32[]{:S(2)}) copy-start(f32[512]{0:T(512)} %param.17) | copy-start | bytes 6148
  96.2 1.5 %collective-permute-start = (f32[256,128]{1,0:T(8,128)S(1)}, f32[256,128]{1,0:T(8,128)S(1)}, u32[]{:S(2)}, u32[]{:S(2)}) collective-permute-start(f32[256,128]{1,0:T(8,128)S(1)} %bitcast.13), channel_id=1, source_target_pairs={{0,1},{1,0},{2,3},{3,2},{4,5},{5,4},{6,7},{7,6},{8,9},{9,8},{10,11... | collective-permute-start | bytes 393224 | tf_op jit(solution)/shard_map/swap/ppermute | solution.py:290

commit v7 on v6

--- a/solution.py
+++ b/solution.py
@@ -11,7 +11,7 @@
 F32 = jnp.float32
 BF16 = jnp.bfloat16
 LANES = 128
-CHUNKS = 4
+CHUNKS = 2
 
 
 def split_np(table):

time: 98.6 us -> 98.6 us (level)
  no operation moved by 1% of the time
where the time goes in v7:
time: 98.6 us; the launch traced here: 98.4 us
  blocking collectives  90.4 us (92%)
  Pallas kernels  6.87 us (7%)
    all_to_all x1, blocking collectives, exchange(): lax.all_to_all(shaped, ('seq', 'dp'), split_axis=0, concat_axis=0, tiled=...  50.7 us
    all_to_all x1, blocking collectives, shards(): lax.all_to_all(shaped, ('seq', 'dp'), split_axis=0, concat_axis=0, tiled=...  39.7 us
    pallas_call x1, Pallas kernels, shards(): pl.pallas_call(lambda *refs: mid_kernel(devices, groups, own, batch, rows...  3.49 us
  transfers between devices with their start and end apart: 1, of which 0 were waited for; matrix products, arithmetic and copies ran while one was open for 0% of the time, Pallas kernels for 1%

profile of v7, /device:TPU:1, one launch (start us, length us, event | category | flops | bytes accessed | tf_op | source)
XLA Modules:
  0.0 98.4 jit_solution(554190998073434612)
XLA Ops:
  0.6 1.4 %pre.1 = f32[2304,128]{1,0:T(8,128)S(1)} custom-call(s32[1]{0:T(128)} %bitcast.refs_0_, bf16[2,512,128]{2,1,0:T(8,128)(2,1)} %refs_2_.4, bf16[2,512,128]{2,1,0:T(8,128)(2,1)} %refs_3_.4, bf16[2,512,128]{2,1,0:T(8,128)(2,1)} %refs_4_.4, bf16[2,512,128]{2,1,0:T(8,128)(2,1)} %refs_5_.4, f32[512,128]{1,0:T(8,128)} %refs_5_.3), custom_call_target="tpu_custom_call" | custom-call | tf_op jit(solution)/shard_map/pre/pallas_call | solution.py:261
  2.0 0.0 copy-start.4
  2.0 0.0 copy-start.5
  2.0 0.0 copy-start.6
  2.0 0.0 copy-start.7
  2.1 0.0 copy-start.8
  2.1 0.0 copy-start.9
  2.1 0.0 copy-start.10
  2.1 50.7 %all_to_all.10 = f32[256,9,1,128]{3,2,1,0:T(1,128)S(1)} all-to-all(f32[256,9,1,128]{3,2,1,0:T(1,128)S(1)} %bitcast.9), channel_id=1, replica_groups=mesh['seq'=64,'dp'=4] {'seq','dp'}, dimensions={0} | all-to-all | bytes 2359296 | tf_op jit(solution)/shard_map/gather/all_to_all | solution.py:256
  52.8 0.0 copy-done.4
  52.8 0.0 copy-done.5
  52.8 0.0 copy-done.6
  52.8 0.0 copy-done.7
  52.8 0.0 copy-done.8
  52.8 0.0 copy-done.9
  52.8 0.0 copy-done.10
  52.8 3.5 %mid.1 = f32[2304,128]{1,0:T(8,128)S(1)} custom-call(f32[2304,128]{1,0:T(8,128)S(1)} %bitcast.10, bf16[256,384]{1,0:T(8,128)(2,1)S(1)} %copy-done.6, bf16[256,192]{1,0:T(8,128)(2,1)S(1)} %copy-done.8, bf16[768,256]{1,0:T(8,128)(2,1)S(1)} %copy-done.4, bf16[768,256]{1,0:T(8,128)(2,1)S(1)} %copy-done.5, bf16[128,768]{1,0:T(8,128)(2,1)S(1)} %copy-done.7, ...), custom_call_target="tpu_custom_call" | custom-call | tf_op jit(solution)/shard_map/mid/pallas_call | solution.py:277
  56.3 0.0 copy-start.11
  56.3 0.0 copy-start
  56.3 0.0 copy-start.1
  56.3 0.0 copy-start.2
  56.3 0.0 copy-start.3
  56.4 39.7 %all_to_all.11 = f32[256,9,1,128]{3,2,1,0:T(1,128)S(1)} all-to-all(f32[256,9,1,128]{3,2,1,0:T(1,128)S(1)} %bitcast.11), channel_id=1, replica_groups=mesh['seq'=64,'dp'=4] {'seq','dp'}, dimensions={0} | all-to-all | bytes 2359296 | tf_op jit(solution)/shard_map/scatter/all_to_all | solution.py:286
  96.1 0.1 slice.4
  96.2 0.1 collective-permute-start
  96.3 0.0 copy-done.11
  96.3 0.0 copy-done
  96.3 0.0 copy-done.1
  96.3 0.0 copy-done.2
  96.3 0.0 copy-done.3
  96.4 1.3 %post.1 = (bf16[2,512,128]{2,1,0:T(8,128)(2,1)}, bf16[2,512,128]{2,1,0:T(8,128)(2,1)}, bf16[2,512,128]{2,1,0:T(8,128)(2,1)}, bf16[2,512,128]{2,1,0:T(8,128)(2,1)}) custom-call(f32[2304,128]{1,0:T(8,128)S(1)} %bitcast.8, f32[2,256]{1,0:T(2,128)S(1)} %reshape.33.refs_1_, bf16[2,512,128]{2,1,0:T(8,128)(2,1)S(1)} %copy-done, bf16[2,512,128]{2,1,0:T(8,128)(2,1)S(1)} %copy-done.1, ...), custom_call_target="tpu_custom_call" | custom-call | flops 1000000 | bytes 4000000 | tf_op jit(solution)/shard_map/post/pallas_call | solution.py:293
  97.6 0.0 collective-permute-done.refs_2_
  97.7 0.7 join.1
  (1 shorter events, 0.0 us)
Async XLA Ops:
  2.0 50.7 %copy-start.4 = (bf16[768,256]{1,0:T(8,128)(2,1)S(1)}, bf16[768,256]{1,0:T(8,128)(2,1)}, u32[]{:S(2)}) copy-start(bf16[768,256]{1,0:T(8,128)(2,1)} %constant.25.clone.refs_3_) | copy-start | bytes 1179652
  2.0 50.7 %copy-start.5 = (bf16[768,256]{1,0:T(8,128)(2,1)S(1)}, bf16[768,256]{1,0:T(8,128)(2,1)}, u32[]{:S(2)}) copy-start(bf16[768,256]{1,0:T(8,128)(2,1)} %constant.26.clone.refs_4_) | copy-start | bytes 1179652
  2.0 50.7 %copy-start.6 = (bf16[256,384]{1,0:T(8,128)(2,1)S(1)}, bf16[256,384]{1,0:T(8,128)(2,1)}, u32[]{:S(2)}) copy-start(bf16[256,384]{1,0:T(8,128)(2,1)} %constant.23.clone.refs_1_) | copy-start | bytes 589828
  2.0 50.7 %copy-start.7 = (bf16[128,768]{1,0:T(8,128)(2,1)S(1)}, bf16[128,768]{1,0:T(8,128)(2,1)}, u32[]{:S(2)}) copy-start(bf16[128,768]{1,0:T(8,128)(2,1)} %constant.27.clone.refs_5_) | copy-start | bytes 589828
  2.1 50.7 %copy-start.8 = (bf16[256,192]{1,0:T(8,128)(2,1)S(1)}, bf16[256,192]{1,0:T(8,128)(2,1)}, u32[]{:S(2)}) copy-start(bf16[256,192]{1,0:T(8,128)(2,1)} %constant.24.clone.refs_2_) | copy-start | bytes 294916
  2.1 50.7 %copy-start.9 = (f32[128,256]{1,0:T(8,128)S(1)}, f32[128,256]{1,0:T(8,128)}, u32[]{:S(2)}) copy-start(f32[128,256]{1,0:T(8,128)} %constant.29.clone.refs_7_) | copy-start | bytes 393220
  2.1 50.7 %copy-start.10 = (bf16[64,768]{1,0:T(8,128)(2,1)S(1)}, bf16[64,768]{1,0:T(8,128)(2,1)}, u32[]{:S(2)}) copy-start(bf16[64,768]{1,0:T(8,128)(2,1)} %constant.28.clone.refs_6_) | copy-start | bytes 294916
  56.3 40.0 %copy-start.11 = (f32[512]{0:T(512)S(1)}, f32[512]{0:T(512)}, u32[]{:S(2)}) copy-start(f32[512]{0:T(512)} %param.17) | copy-start | bytes 6148
  56.3 40.0 %copy-start = (bf16[2,512,128]{2,1,0:T(8,128)(2,1)S(1)}, bf16[2,512,128]{2,1,0:T(8,128)(2,1)}, u32[]{:S(2)}) copy-start(bf16[2,512,128]{2,1,0:T(8,128)(2,1)} %refs_2_.4) | copy-start | bytes 786436
  56.3 40.0 %copy-start.1 = (bf16[2,512,128]{2,1,0:T(8,128)(2,1)S(1)}, bf16[2,512,128]{2,1,0:T(8,128)(2,1)}, u32[]{:S(2)}) copy-start(bf16[2,512,128]{2,1,0:T(8,128)(2,1)} %refs_3_.4) | copy-start | bytes 786436
  56.3 40.0 %copy-start.2 = (bf16[2,512,128]{2,1,0:T(8,128)(2,1)S(1)}, bf16[2,512,128]{2,1,0:T(8,128)(2,1)}, u32[]{:S(2)}) copy-start(bf16[2,512,128]{2,1,0:T(8,128)(2,1)} %refs_4_.4) | copy-start | bytes 786436
  56.3 40.0 %copy-start.3 = (bf16[2,512,128]{2,1,0:T(8,128)(2,1)S(1)}, bf16[2,512,128]{2,1,0:T(8,128)(2,1)}, u32[]{:S(2)}) copy-start(bf16[2,512,128]{2,1,0:T(8,128)(2,1)} %refs_5_.4) | copy-start | bytes 786436
  96.2 1.5 %collective-permute-start = (f32[256,128]{1,0:T(8,128)S(1)}, f32[256,128]{1,0:T(8,128)S(1)}, u32[]{:S(2)}, u32[]{:S(2)}) collective-permute-start(f32[256,128]{1,0:T(8,128)S(1)} %bitcast.12), channel_id=1, source_target_pairs={{0,1},{1,0},{2,3},{3,2},{4,5},{5,4},{6,7},{7,6},{8,9},{9,8},{10,11... | collective-permute-start | bytes 393224 | tf_op jit(solution)/shard_map/swap/ppermute | solution.py:290

commit v8 on v7

--- a/solution.py
+++ b/solution.py
@@ -108,14 +108,6 @@
     send[pl.ds(2 * batch * own, peers, stride=rows), :] = row
 
 
-def leave_product(table, data):
-    depth = data.shape[0]
-    high = data.astype(BF16)
-    low = (data - high.astype(F32)).astype(BF16)
-    first = table[:, :depth]
-    return mm(first, high) + mm(first, low) + mm(table[:, 2 * depth :], high)
-
-
 def mid_kernel(
     devices, groups, own, batch, rows_in, rows_out, r_ref, enter, enter_real, lane_fwd, lane_inv,
     leave, leave_real, turn_ref, send_ref,
@@ -141,7 +133,7 @@
         turned = [
             twist_back(spread[i * K1 : (i + 1) * K1], turn_cos, turn_sin) for i in range(count)
         ]
-        return leave_product(table[...], jnp.concatenate(turned, 1))
+        return mm(table[...], parts(jnp.concatenate(turned, 1), 0))
 
     def pair(spec, i):
         rows = spec[i * K1 : (i + 1) * K1]

time: 98.6 us -> 98.5 us (level)
  no operation moved by 1% of the time
where the time goes in v8:
time: 98.5 us; the launch traced here: 98.4 us
  blocking collectives  90.4 us (92%)
  Pallas kernels  6.84 us (7%)
    all_to_all x1, blocking collectives, exchange(): lax.all_to_all(shaped, ('seq', 'dp'), split_axis=0, concat_axis=0, tiled=...  50.7 us
    all_to_all x1, blocking collectives, shards(): lax.all_to_all(shaped, ('seq', 'dp'), split_axis=0, concat_axis=0, tiled=...  39.7 us
    pallas_call x1, Pallas kernels, shards(): pl.pallas_call(lambda *refs: mid_kernel(devices, groups, own, batch, rows...  3.46 us
  transfers between devices with their start and end apart: 1, of which 0 were waited for; matrix products, arithmetic and copies ran while one was open for 0% of the time, Pallas kernels for 1%

profile of v8, /device:TPU:1, one launch (start us, length us, event | category | flops | bytes accessed | tf_op | source)
XLA Modules:
  0.0 98.4 jit_solution(13559949594119709869)
XLA Ops:
  0.6 1.4 %pre.1 = f32[2304,128]{1,0:T(8,128)S(1)} custom-call(s32[1]{0:T(128)} %bitcast.refs_0_, bf16[2,512,128]{2,1,0:T(8,128)(2,1)} %refs_2_.4, bf16[2,512,128]{2,1,0:T(8,128)(2,1)} %refs_3_.4, bf16[2,512,128]{2,1,0:T(8,128)(2,1)} %refs_4_.4, bf16[2,512,128]{2,1,0:T(8,128)(2,1)} %refs_5_.4, f32[512,128]{1,0:T(8,128)} %refs_5_.3), custom_call_target="tpu_custom_call" | custom-call | tf_op jit(solution)/shard_map/pre/pallas_call | solution.py:253
  2.0 0.0 copy-start.4
  2.0 0.0 copy-start.5
  2.0 0.0 copy-start.6
  2.0 0.0 copy-start.7
  2.1 0.0 copy-start.8
  2.1 0.0 copy-start.9
  2.1 0.0 copy-start.10
  2.1 50.7 %all_to_all.10 = f32[256,9,1,128]{3,2,1,0:T(1,128)S(1)} all-to-all(f32[256,9,1,128]{3,2,1,0:T(1,128)S(1)} %bitcast.9), channel_id=1, replica_groups=mesh['seq'=64,'dp'=4] {'seq','dp'}, dimensions={0} | all-to-all | bytes 2359296 | tf_op jit(solution)/shard_map/gather/all_to_all | solution.py:248
  52.8 0.0 copy-done.4
  52.8 0.0 copy-done.5
  52.8 0.0 copy-done.6
  52.8 0.0 copy-done.7
  52.8 0.0 copy-done.8
  52.8 0.0 copy-done.9
  52.8 0.0 copy-done.10
  52.8 3.5 %mid.1 = f32[2304,128]{1,0:T(8,128)S(1)} custom-call(f32[2304,128]{1,0:T(8,128)S(1)} %bitcast.10, bf16[256,384]{1,0:T(8,128)(2,1)S(1)} %copy-done.6, bf16[256,192]{1,0:T(8,128)(2,1)S(1)} %copy-done.8, bf16[768,256]{1,0:T(8,128)(2,1)S(1)} %copy-done.4, bf16[768,256]{1,0:T(8,128)(2,1)S(1)} %copy-done.5, bf16[128,768]{1,0:T(8,128)(2,1)S(1)} %copy-done.7, ...), custom_call_target="tpu_custom_call" | custom-call | tf_op jit(solution)/shard_map/mid/pallas_call | solution.py:269
  56.3 0.0 copy-start.11
  56.3 0.0 copy-start
  56.3 0.0 copy-start.1
  56.3 0.0 copy-start.2
  56.3 0.0 copy-start.3
  56.3 39.7 %all_to_all.11 = f32[256,9,1,128]{3,2,1,0:T(1,128)S(1)} all-to-all(f32[256,9,1,128]{3,2,1,0:T(1,128)S(1)} %bitcast.11), channel_id=1, replica_groups=mesh['seq'=64,'dp'=4] {'seq','dp'}, dimensions={0} | all-to-all | bytes 2359296 | tf_op jit(solution)/shard_map/scatter/all_to_all | solution.py:278
  96.1 0.1 slice.4
  96.2 0.1 collective-permute-start
  96.3 0.0 copy-done.11
  96.3 0.0 copy-done
  96.3 0.0 copy-done.1
  96.3 0.0 copy-done.2
  96.3 0.0 copy-done.3
  96.3 1.3 %post.1 = (bf16[2,512,128]{2,1,0:T(8,128)(2,1)}, bf16[2,512,128]{2,1,0:T(8,128)(2,1)}, bf16[2,512,128]{2,1,0:T(8,128)(2,1)}, bf16[2,512,128]{2,1,0:T(8,128)(2,1)}) custom-call(f32[2304,128]{1,0:T(8,128)S(1)} %bitcast.8, f32[2,256]{1,0:T(2,128)S(1)} %reshape.33.refs_1_, bf16[2,512,128]{2,1,0:T(8,128)(2,1)S(1)} %copy-done, bf16[2,512,128]{2,1,0:T(8,128)(2,1)S(1)} %copy-done.1, ...), custom_call_target="tpu_custom_call" | custom-call | flops 1000000 | bytes 4000000 | tf_op jit(solution)/shard_map/post/pallas_call | solution.py:285
  97.6 0.0 collective-permute-done.refs_2_
  97.6 0.7 join.1
  (1 shorter events, 0.0 us)
Async XLA Ops:
  2.0 50.7 %copy-start.4 = (bf16[768,256]{1,0:T(8,128)(2,1)S(1)}, bf16[768,256]{1,0:T(8,128)(2,1)}, u32[]{:S(2)}) copy-start(bf16[768,256]{1,0:T(8,128)(2,1)} %constant.25.clone.refs_3_) | copy-start | bytes 1179652
  2.0 50.7 %copy-start.5 = (bf16[768,256]{1,0:T(8,128)(2,1)S(1)}, bf16[768,256]{1,0:T(8,128)(2,1)}, u32[]{:S(2)}) copy-start(bf16[768,256]{1,0:T(8,128)(2,1)} %constant.26.clone.refs_4_) | copy-start | bytes 1179652
  2.0 50.7 %copy-start.6 = (bf16[256,384]{1,0:T(8,128)(2,1)S(1)}, bf16[256,384]{1,0:T(8,128)(2,1)}, u32[]{:S(2)}) copy-start(bf16[256,384]{1,0:T(8,128)(2,1)} %constant.23.clone.refs_1_) | copy-start | bytes 589828
  2.0 50.7 %copy-start.7 = (bf16[128,768]{1,0:T(8,128)(2,1)S(1)}, bf16[128,768]{1,0:T(8,128)(2,1)}, u32[]{:S(2)}) copy-start(bf16[128,768]{1,0:T(8,128)(2,1)} %constant.27.clone.refs_5_) | copy-start | bytes 589828
  2.1 50.7 %copy-start.8 = (bf16[256,192]{1,0:T(8,128)(2,1)S(1)}, bf16[256,192]{1,0:T(8,128)(2,1)}, u32[]{:S(2)}) copy-start(bf16[256,192]{1,0:T(8,128)(2,1)} %constant.24.clone.refs_2_) | copy-start | bytes 294916
  2.1 50.7 %copy-start.9 = (f32[128,256]{1,0:T(8,128)S(1)}, f32[128,256]{1,0:T(8,128)}, u32[]{:S(2)}) copy-start(f32[128,256]{1,0:T(8,128)} %constant.29.clone.refs_7_) | copy-start | bytes 393220
  2.1 50.7 %copy-start.10 = (bf16[64,768]{1,0:T(8,128)(2,1)S(1)}, bf16[64,768]{1,0:T(8,128)(2,1)}, u32[]{:S(2)}) copy-start(bf16[64,768]{1,0:T(8,128)(2,1)} %constant.28.clone.refs_6_) | copy-start | bytes 294916
  56.3 40.0 %copy-start.11 = (f32[512]{0:T(512)S(1)}, f32[512]{0:T(512)}, u32[]{:S(2)}) copy-start(f32[512]{0:T(512)} %param.17) | copy-start | bytes 6148
  56.3 40.0 %copy-start = (bf16[2,512,128]{2,1,0:T(8,128)(2,1)S(1)}, bf16[2,512,128]{2,1,0:T(8,128)(2,1)}, u32[]{:S(2)}) copy-start(bf16[2,512,128]{2,1,0:T(8,128)(2,1)} %refs_2_.4) | copy-start | bytes 786436
  56.3 40.0 %copy-start.1 = (bf16[2,512,128]{2,1,0:T(8,128)(2,1)S(1)}, bf16[2,512,128]{2,1,0:T(8,128)(2,1)}, u32[]{:S(2)}) copy-start(bf16[2,512,128]{2,1,0:T(8,128)(2,1)} %refs_3_.4) | copy-start | bytes 786436
  56.3 40.0 %copy-start.2 = (bf16[2,512,128]{2,1,0:T(8,128)(2,1)S(1)}, bf16[2,512,128]{2,1,0:T(8,128)(2,1)}, u32[]{:S(2)}) copy-start(bf16[2,512,128]{2,1,0:T(8,128)(2,1)} %refs_4_.4) | copy-start | bytes 786436
  56.3 40.0 %copy-start.3 = (bf16[2,512,128]{2,1,0:T(8,128)(2,1)S(1)}, bf16[2,512,128]{2,1,0:T(8,128)(2,1)}, u32[]{:S(2)}) copy-start(bf16[2,512,128]{2,1,0:T(8,128)(2,1)} %refs_5_.4) | copy-start | bytes 786436
  96.2 1.5 %collective-permute-start = (f32[256,128]{1,0:T(8,128)S(1)}, f32[256,128]{1,0:T(8,128)S(1)}, u32[]{:S(2)}, u32[]{:S(2)}) collective-permute-start(f32[256,128]{1,0:T(8,128)S(1)} %bitcast.12), channel_id=1, source_target_pairs={{0,1},{1,0},{2,3},{3,2},{4,5},{5,4},{6,7},{7,6},{8,9},{9,8},{10,11... | collective-permute-start | bytes 393224 | tf_op jit(solution)/shard_map/swap/ppermute | solution.py:282
